TPU v7x, 128 devices: a whole 4x4x4 slice. The times are simulated.
128 devices in a mesh: frame: 16 (over x, z), inframe: 8 (over y, core).
Axes of the slice: x: 4, y: 4, z: 4, core: 2. Of those that a mesh axis runs over, the one named last changes fastest.
Arguments:
- tokens: bfloat16 [96, 1024, 1152], P('frame', 'inframe'), may hold values from -6 to 6
- clip_ids: int32 [96], replicated, may hold values from 0 to 3, never falling along the last dimension, each value on 1 to 48 neighbouring positions
- modulation: float32 [4, 6, 1152], replicated, may hold values from -3 to 3
- w_spatial_qkv: bfloat16 [1152, 3456], replicated, may hold values from -3 to 3
- w_spatial_out: bfloat16 [1152, 1152], replicated, may hold values from -0.1875 to 0.1875
- w_temporal_qkv: bfloat16 [1152, 3456], replicated, may hold values from -3 to 3
- w_temporal_out: bfloat16 [1152, 1152], replicated, may hold values from -0.1875 to 0.1875
Outputs:
- block_out: bfloat16 [96, 1024, 1152], P('frame', 'inframe')
Inputs may be any that keep to these rules, and one draw needn't show every extreme that they name: `clip_ids`: clip numbers never fall along the frames; every clip holds 1 to 48 frames, and one clip exactly that many.
All inputs are finite; a program needn't handle non-finite values.
Results may differ from a plain program's by a relative error of at most 0.0085.
Values may be sent and summed in bfloat16 or wider, within the bound.
A program may use at most 192 MiB of HBM per device.

v0:
```python
import jax
import jax.numpy as jnp
from jax import lax
from jax.sharding import PartitionSpec as P

HEADS = 16


def norm_mod(x, shift, scale):
    values = x.astype(jnp.float32)
    center = values - jnp.mean(values, axis=-1, keepdims=True)
    spread = jnp.mean(center * center, axis=-1, keepdims=True)
    return (center * lax.rsqrt(spread + 1e-06) * (1.0 + scale) + shift).astype(jnp.bfloat16)


def softmax_last(scores):
    top = jnp.max(scores, axis=-1, keepdims=True)
    powers = jnp.exp(scores - top)
    return powers / jnp.sum(powers, axis=-1, keepdims=True)


def project(hidden, weight):
    width = weight.shape[0]
    flat = jnp.dot(hidden.reshape(-1, width), weight, preferred_element_type=jnp.float32).astype(
        jnp.bfloat16
    )
    joined = flat.reshape(hidden.shape[:-1] + (weight.shape[1],))
    return (joined[..., :width], joined[..., width : 2 * width], joined[..., 2 * width :])


def body(
    tokens, clip_ids, modulation, w_spatial_qkv, w_spatial_out, w_temporal_qkv, w_temporal_out
):
    frames_dev, rows, width = tokens.shape
    head_size = width // HEADS
    factor = head_size ** (-0.5)
    start = lax.axis_index("frame") * frames_dev
    own_clips = lax.dynamic_slice_in_dim(clip_ids, start, frames_dev)
    table = (
        own_clips[:, None] == jnp.arange(modulation.shape[0], dtype=jnp.int32)[None, :]
    ).astype(jnp.float32)
    mods = jnp.einsum("fc,ckd->fkd", table, modulation, precision=lax.Precision.HIGHEST)
    hidden = norm_mod(tokens, mods[:, 0][:, None], mods[:, 1][:, None])
    query, keys, values = project(hidden, w_spatial_qkv)
    q_part = lax.all_to_all(query, "inframe", split_axis=2, concat_axis=1, tiled=True)
    k_part = lax.all_to_all(keys, "inframe", split_axis=2, concat_axis=1, tiled=True)
    v_part = lax.all_to_all(values, "inframe", split_axis=2, concat_axis=1, tiled=True)
    count, seq, cols = q_part.shape
    local = cols // head_size
    q_heads = q_part.reshape(count, seq, local, head_size)
    k_heads = k_part.reshape(count, seq, local, head_size)
    v_heads = v_part.reshape(count, seq, local, head_size)
    scores = (
        jnp.einsum("fqhe,fkhe->fhqk", q_heads, k_heads, preferred_element_type=jnp.float32) * factor
    )
    probs = softmax_last(scores).astype(jnp.bfloat16)
    mixed = jnp.einsum(
        "fhqk,fkhe->fqhe", probs, v_heads, preferred_element_type=jnp.float32
    ).astype(jnp.bfloat16)
    mixed = mixed.reshape(count, seq, cols)
    back = lax.all_to_all(mixed, "inframe", split_axis=1, concat_axis=2, tiled=True)
    proj = jnp.dot(
        back.reshape(-1, width), w_spatial_out, preferred_element_type=jnp.float32
    ).reshape(tokens.shape)
    first = (tokens.astype(jnp.float32) + mods[:, 2][:, None] * proj).astype(jnp.bfloat16)
    hidden_two = norm_mod(first, mods[:, 3][:, None], mods[:, 4][:, None])
    q_own, k_own, v_own = project(hidden_two, w_temporal_qkv)
    q_all, k_all, v_all = (
        lax.all_to_all(q_own, "frame", split_axis=1, concat_axis=0, tiled=True),
        lax.all_to_all(k_own, "frame", split_axis=1, concat_axis=0, tiled=True),
        lax.all_to_all(v_own, "frame", split_axis=1, concat_axis=0, tiled=True),
    )
    total_frames, spots, _ = q_all.shape
    q_heads = q_all.reshape(total_frames, spots, HEADS, head_size)
    k_heads = k_all.reshape(total_frames, spots, HEADS, head_size)
    v_heads = v_all.reshape(total_frames, spots, HEADS, head_size)
    scores = (
        jnp.einsum("fphe,gphe->phfg", q_heads, k_heads, preferred_element_type=jnp.float32) * factor
    )
    same = clip_ids[:, None] == clip_ids[None, :]
    scores = jnp.where(same[None, None], scores, jnp.float32(-1e30))
    probs = softmax_last(scores).astype(jnp.bfloat16)
    mixed_two = jnp.einsum(
        "phfg,gphe->fphe", probs, v_heads, preferred_element_type=jnp.float32
    ).astype(jnp.bfloat16)
    mixed_two = mixed_two.reshape(total_frames, spots, width)
    back_two = lax.all_to_all(mixed_two, "frame", split_axis=0, concat_axis=1, tiled=True)
    proj_two = jnp.dot(
        back_two.reshape(-1, width), w_temporal_out, preferred_element_type=jnp.float32
    ).reshape(tokens.shape)
    return (first.astype(jnp.float32) + mods[:, 5][:, None] * proj_two).astype(jnp.bfloat16)


def solution(mesh):
    in_specs = (P("frame", "inframe", None), P(), P(), P(), P(), P(), P())
    out_specs = P("frame", "inframe", None)
    return jax.shard_map(body, mesh=mesh, in_specs=in_specs, out_specs=out_specs, check_vma=False)
```

profile of v0, /device:TPU:0, one launch (start us, length us, event | category | flops | bytes accessed | tf_op | source)
XLA Modules:
  0.0 424.2 jit_solution(1478233581070488511)
XLA Ops:
  5.9 9.8 %convolution_convert_fusion.1 = bf16[768,3456]{1,0:T(8,128)(2,1)S(1)} fusion(bf16[768,1152]{1,0:T(8,128)(2,1)S(1)} %bitcast.98, bf16[1152,3456]{1,0:T(8,128)(2,1)} %param.10), kind=kOutput, calls=%fused_computation.10 | convolution fusion | flops 6117949440 | bytes 15040512 | tf_op jit(solution)/shard_map/dot_general | solution.py:24
  15.7 2.6 fusion.50
  18.3 4.2 copy.90
  22.5 4.5 %all-to-all-start = ((bf16[6,128,1152]{1,0,2:T(8,128)(2,1)}), bf16[6,128,1152]{1,0,2:T(8,128)(2,1)}, u32[]{:S(2)}, u32[]{:S(2)}) async-start(bf16[6,128,1152]{1,0,2:T(8,128)(2,1)} %copy.90), calls=%async_computation | async-start | bytes 4718592 | tf_op jit(solution)/shard_map/all_to_all | solution.py:47
  27.1 4.3 %copy.91 = bf16[6,128,1152]{1,0,2:T(8,128)(2,1)} copy(bf16[6,128,1152]{2,1,0:T(8,128)(2,1)} %get-tuple-element.9) | data formatting | bytes 3538944
  31.3 25.8 %all-to-all-done = bf16[6,128,1152]{1,0,2:T(8,128)(2,1)} async-done(((bf16[6,128,1152]{1,0,2:T(8,128)(2,1)}), bf16[6,128,1152]{1,0,2:T(8,128)(2,1)}, u32[]{:S(2)}, u32[]{:S(2)}) %all-to-all-start) | async-done | bytes 1769504 | tf_op jit(solution)/shard_map/all_to_all | solution.py:47
  57.2 4.4 %all-to-all-start.1 = ((bf16[6,128,1152]{1,0,2:T(8,128)(2,1)}), bf16[6,128,1152]{1,0,2:T(8,128)(2,1)}, u32[]{:S(2)}, u32[]{:S(2)}) async-start(bf16[6,128,1152]{1,0,2:T(8,128)(2,1)} %copy.91), calls=%async_computation.1 | async-start | bytes 4718592 | tf_op jit(solution)/shard_map/all_to_all | solution.py:45
  61.6 4.2 copy.92
  65.8 25.8 %all-to-all-done.1 = bf16[6,128,1152]{1,0,2:T(8,128)(2,1)} async-done(((bf16[6,128,1152]{1,0,2:T(8,128)(2,1)}), bf16[6,128,1152]{1,0,2:T(8,128)(2,1)}, u32[]{:S(2)}, u32[]{:S(2)}) %all-to-all-start.1) | async-done | bytes 1769504 | tf_op jit(solution)/shard_map/all_to_all | solution.py:45
  91.6 4.6 %all-to-all-start.2 = ((bf16[6,128,1152]{1,0,2:T(8,128)(2,1)}), bf16[6,128,1152]{1,0,2:T(8,128)(2,1)}, u32[]{:S(2)}, u32[]{:S(2)}) async-start(bf16[6,128,1152]{1,0,2:T(8,128)(2,1)} %copy.92), calls=%async_computation.2 | async-start | bytes 4718592 | tf_op jit(solution)/shard_map/all_to_all | solution.py:46
  96.2 4.0 copy.52
  100.2 3.8 reshape.110
  104.0 4.0 copy.55
  108.0 3.8 reshape.111
  111.8 14.4 %all-to-all-done.2 = bf16[6,128,1152]{1,0,2:T(8,128)(2,1)} async-done(((bf16[6,128,1152]{1,0,2:T(8,128)(2,1)}), bf16[6,128,1152]{1,0,2:T(8,128)(2,1)}, u32[]{:S(2)}, u32[]{:S(2)}) %all-to-all-start.2) | async-done | bytes 1769504 | tf_op jit(solution)/shard_map/all_to_all | solution.py:46
  126.2 4.0 copy.58
  130.2 3.8 reshape.112
  134.0 23.8 %fusion.51 = (f32[6,2,1024]{2,1,0:T(2,128)S(1)}, f32[6,2,1024,1024]{2,3,1,0:T(8,128)}) fusion(bf16[6,1024,2,72]{1,3,2,0:T(8,128)(2,1)} %reshape.111, bf16[6,1024,2,72]{1,3,2,0:T(8,128)(2,1)} %reshape.112), kind=kOutput, calls=%fused_computation.73 | convolution fusion | flops 1849689088 | bytes 53919744 | tf_op jit(solution)/shard_map/sub | solution.py:18
  157.8 18.6 %fusion.39 = bf16[6,2,72,1024]{3,2,1,0:T(8,128)(2,1)} fusion(bf16[6,1024,2,72]{1,3,2,0:T(8,128)(2,1)} %reshape.110, f32[6,2,1024,1024]{2,3,1,0:T(8,128)} %get-tuple-element.18, f32[6,2,1024]{2,1,0:T(2,128)S(1)} %get-tuple-element.17), kind=kOutput, calls=%fused_computation.50 | convolution fusion | flops 1837989888 | bytes 53919744 | tf_op jit(solution)/shard_map/fhqk,fkhe->fqhe/dot_general | solution.py:57
  176.4 6.0 %copy.60 = bf16[6,1024,144]{2,0,1:T(8,128)(2,1)} copy(bf16[6,1024,144]{1,2,0:T(8,128)(2,1)} %bitcast.102) | data formatting | bytes 3538944 | tf_op jit(solution)/shard_map/reshape | solution.py:60
  182.4 8.8 %reshape.123 = bf16[8,2,55296]{2,1,0:T(2,128)(2,1)} reshape(bf16[1024,6,144]{2,1,0:T(8,128)(2,1)} %bitcast.93) | data formatting | bytes 3538944
  191.2 28.2 %all_to_all.120 = bf16[8,2,55296]{2,1,0:T(2,128)(2,1)} all-to-all(bf16[8,2,55296]{2,1,0:T(2,128)(2,1)} %reshape.123), channel_id=1, replica_groups=mesh['frame'=16,'inframe'=8] {'inframe'}, dimensions={0} | all-to-all | bytes 3538944 | tf_op jit(solution)/shard_map/all_to_all | solution.py:61
  219.4 8.8 %reshape.124 = bf16[1024,6,144]{2,1,0:T(8,128)(2,1)} reshape(bf16[8,2,55296]{2,1,0:T(2,128)(2,1)} %all_to_all.120) | data formatting | bytes 3538944
  228.3 5.3 %copy.62 = bf16[6,128,8,144]{1,3,2,0:T(8,128)(2,1)} copy(bf16[6,128,8,144]{3,0,1,2:T(8,128)(2,1)} %bitcast.94) | data formatting | bytes 3538944 | tf_op jit(solution)/shard_map/all_to_all | solution.py:61
  233.6 5.2 %convert_reduce_fusion = (f32[6,128]{1,0:T(8,128)S(1)}, bf16[6,128,1152]{2,1,0:T(8,128)(2,1)S(1)}) fusion(bf16[6,128,1152]{1,2,0:T(8,128)(2,1)} %bitcast.99, bf16[1152,1152]{1,0:T(8,128)(2,1)S(1)} %copy-done, f32[6,1152]{1,0:T(8,128)S(1)} %get-tuple-element.16, bf16[6,128,1152]{2,1,0:T(8,128)(2,1)} %param.7), kind=kOutput, calls=%fused_computation.16 | convolution fusion | flops 2043739392 | bytes 7993344 | tf_op jit(solution)/shard_map/dot_general | solution.py:62
  241.3 7.4 %convolution_convert_fusion = bf16[768,3456]{1,0:T(8,128)(2,1)S(1)} fusion(bf16[768,1152]{1,0:T(8,128)(2,1)S(1)} %bitcast.100, bf16[1152,3456]{1,0:T(8,128)(2,1)S(1)} %bitcast.104), kind=kOutput, calls=%fused_computation.9 | convolution fusion | flops 6117949440 | bytes 15040512 | tf_op jit(solution)/shard_map/dot_general | solution.py:24
  248.7 2.3 fusion.49
  251.0 2.4 copy.95
  253.4 8.3 %all-to-all-start.6 = ((bf16[6,128,1152]{2,0,1:T(8,128)(2,1)}), bf16[6,128,1152]{2,0,1:T(8,128)(2,1)}, u32[]{:S(2)}, u32[]{:S(2)}) async-start(bf16[6,128,1152]{2,0,1:T(8,128)(2,1)} %copy.95), calls=%async_computation.6 | async-start | bytes 4718592 | tf_op jit(solution)/shard_map/all_to_all | solution.py:70
  261.8 4.0 copy.94
  265.8 29.2 %all-to-all-done.6 = bf16[6,128,1152]{2,0,1:T(8,128)(2,1)} async-done(((bf16[6,128,1152]{2,0,1:T(8,128)(2,1)}), bf16[6,128,1152]{2,0,1:T(8,128)(2,1)}, u32[]{:S(2)}, u32[]{:S(2)}) %all-to-all-start.6) | async-done | bytes 1769504 | tf_op jit(solution)/shard_map/all_to_all | solution.py:70
  295.0 4.4 %all-to-all-start.5 = ((bf16[6,128,1152]{2,0,1:T(8,128)(2,1)}), bf16[6,128,1152]{2,0,1:T(8,128)(2,1)}, u32[]{:S(2)}, u32[]{:S(2)}) async-start(bf16[6,128,1152]{2,0,1:T(8,128)(2,1)} %copy.94), calls=%async_computation.5 | async-start | bytes 4718592 | tf_op jit(solution)/shard_map/all_to_all | solution.py:69
  299.4 3.9 copy.93
  303.4 26.2 %all-to-all-done.5 = bf16[6,128,1152]{2,0,1:T(8,128)(2,1)} async-done(((bf16[6,128,1152]{2,0,1:T(8,128)(2,1)}), bf16[6,128,1152]{2,0,1:T(8,128)(2,1)}, u32[]{:S(2)}, u32[]{:S(2)}) %all-to-all-start.5) | async-done | bytes 1769504 | tf_op jit(solution)/shard_map/all_to_all | solution.py:69
  329.5 4.8 %all-to-all-start.4 = ((bf16[6,128,1152]{2,0,1:T(8,128)(2,1)}), bf16[6,128,1152]{2,0,1:T(8,128)(2,1)}, u32[]{:S(2)}, u32[]{:S(2)}) async-start(bf16[6,128,1152]{2,0,1:T(8,128)(2,1)} %copy.93), calls=%async_computation.4 | async-start | bytes 4718592 | tf_op jit(solution)/shard_map/all_to_all | solution.py:71
  334.5 3.1 copy.72
  337.6 7.7 %reshape.118 = bf16[96,8,16,72]{3,2,1,0:T(8,128)(2,1)} reshape(bf16[16,6,8,1152]{3,2,1,0:T(8,128)(2,1)} %copy.72) | data formatting | bytes 3538944 | tf_op jit(solution)/shard_map/reshape | solution.py:75
  345.3 3.1 copy.69
  348.4 7.6 %reshape.117 = bf16[96,8,16,72]{3,2,1,0:T(8,128)(2,1)} reshape(bf16[16,6,8,1152]{3,2,1,0:T(8,128)(2,1)} %copy.69) | data formatting | bytes 3538944 | tf_op jit(solution)/shard_map/reshape | solution.py:74
  356.0 8.5 %all-to-all-done.4 = bf16[6,128,1152]{2,0,1:T(8,128)(2,1)} async-done(((bf16[6,128,1152]{2,0,1:T(8,128)(2,1)}), bf16[6,128,1152]{2,0,1:T(8,128)(2,1)}, u32[]{:S(2)}, u32[]{:S(2)}) %all-to-all-start.4) | async-done | bytes 1769504 | tf_op jit(solution)/shard_map/all_to_all | solution.py:71
  364.6 3.1 copy.66
  367.7 7.8 %reshape.116 = bf16[96,8,16,72]{3,2,1,0:T(8,128)(2,1)} reshape(bf16[16,6,8,1152]{3,2,1,0:T(8,128)(2,1)} %copy.66) | data formatting | bytes 3538944 | tf_op jit(solution)/shard_map/reshape | solution.py:76
  375.5 6.8 %fusion.26 = f32[8,16,96,96]{2,3,1,0:T(8,128)S(1)} fusion(bf16[96,8,16,72]{3,2,1,0:T(8,128)(2,1)} %reshape.118, bf16[96,8,16,72]{3,2,1,0:T(8,128)(2,1)} %reshape.117), kind=kOutput, calls=%fused_computation.39 | convolution fusion | flops 169869312 | bytes 8257536 | tf_op jit(solution)/shard_map/fphe,gphe->phfg/dot_general | solution.py:78
  382.2 1.9 fusion.52
  384.1 4.4 %fusion.34 = bf16[8,16,72,96]{3,2,1,0:T(8,128)(2,1)} fusion(f32[8,16,96,96]{2,3,1,0:T(8,128)S(1)} %get-tuple-element.22, f32[8,16,96]{2,1,0:T(8,128)S(1)} %get-tuple-element.21, bf16[96,8,16,72]{3,2,1,0:T(8,128)(2,1)S(1)} %copy-done.4), kind=kOutput, calls=%fused_computation.47 | convolution fusion | flops 173113344 | bytes 8306688 | tf_op jit(solution)/shard_map/phfg,gphe->fphe/dot_general | solution.py:83
  388.6 4.2 copy.77
  392.8 25.6 %all_to_all.121 = bf16[96,8,1152]{2,1,0:T(8,128)(2,1)S(1)} all-to-all(bf16[96,8,1152]{2,1,0:T(8,128)(2,1)} %copy.77), channel_id=1, replica_groups=mesh['frame'=16,'inframe'=8] {'frame'}, dimensions={0} | all-to-all | bytes 3538944 | tf_op jit(solution)/shard_map/all_to_all | solution.py:87
  418.4 5.6 %fusion.23 = bf16[6,128,1152]{2,1,0:T(8,128)(2,1)} fusion(bf16[6,128,1152]{2,1,0:T(8,128)(2,1)S(1)} %copy-done.3, bf16[1152,1152]{1,0:T(8,128)(2,1)} %param.13, bf16[6,16,8,1152]{3,2,0,1:T(8,128)(2,1)S(1)} %bitcast.101, f32[6,1152]{1,0:T(8,128)S(1)} %get-tuple-element.11), kind=kOutput, calls=%fused_computation.36 | convolution fusion | flops 2041970688 | bytes 7990272 | tf_op jit(solution)/shard_map/dot_general | solution.py:88
  (30 shorter events, 8.4 us)
Async XLA Ops:
  0.0 233.6 %copy-start = (bf16[1152,1152]{1,0:T(8,128)(2,1)S(1)}, bf16[1152,1152]{1,0:T(8,128)(2,1)}, u32[]{:S(2)}) copy-start(bf16[1152,1152]{1,0:T(8,128)(2,1)} %param.11) | copy-start | bytes 7962628
  0.0 4.0 copy-start.1
  22.5 34.7 %all-to-all-start = ((bf16[6,128,1152]{1,0,2:T(8,128)(2,1)}), bf16[6,128,1152]{1,0,2:T(8,128)(2,1)}, u32[]{:S(2)}, u32[]{:S(2)}) async-start(bf16[6,128,1152]{1,0,2:T(8,128)(2,1)} %copy.90), calls=%async_computation | async-start | bytes 4718592 | tf_op jit(solution)/shard_map/all_to_all | solution.py:47
  57.2 34.4 %all-to-all-start.1 = ((bf16[6,128,1152]{1,0,2:T(8,128)(2,1)}), bf16[6,128,1152]{1,0,2:T(8,128)(2,1)}, u32[]{:S(2)}, u32[]{:S(2)}) async-start(bf16[6,128,1152]{1,0,2:T(8,128)(2,1)} %copy.91), calls=%async_computation.1 | async-start | bytes 4718592 | tf_op jit(solution)/shard_map/all_to_all | solution.py:45
  91.6 34.6 %all-to-all-start.2 = ((bf16[6,128,1152]{1,0,2:T(8,128)(2,1)}), bf16[6,128,1152]{1,0,2:T(8,128)(2,1)}, u32[]{:S(2)}, u32[]{:S(2)}) async-start(bf16[6,128,1152]{1,0,2:T(8,128)(2,1)} %copy.92), calls=%async_computation.2 | async-start | bytes 4718592 | tf_op jit(solution)/shard_map/all_to_all | solution.py:46
  233.6 7.7 %slice-start = ((s8[7962624]{0:T(1024)(128)(4,1)}), s8[4194304]{0:T(1024)(128)(4,1)S(1)}, s32[]{:S(2)}) async-start(s8[7962624]{0:T(1024)(128)(4,1)} %bitcast.103), calls=%async_computation.8 | async-start | bytes 8388608
  233.6 7.7 %slice-start.1 = ((s8[7962624]{0:T(1024)(128)(4,1)}), s8[3768320]{0:T(1024)(128)(4,1)S(1)}, s32[]{:S(2)}) async-start(s8[7962624]{0:T(1024)(128)(4,1)} %bitcast.103), calls=%async_computation.9 | async-start | bytes 7536640
  238.8 1.2 copy-start.2
  253.4 41.5 %all-to-all-start.6 = ((bf16[6,128,1152]{2,0,1:T(8,128)(2,1)}), bf16[6,128,1152]{2,0,1:T(8,128)(2,1)}, u32[]{:S(2)}, u32[]{:S(2)}) async-start(bf16[6,128,1152]{2,0,1:T(8,128)(2,1)} %copy.95), calls=%async_computation.6 | async-start | bytes 4718592 | tf_op jit(solution)/shard_map/all_to_all | solution.py:70
  295.0 34.6 %all-to-all-start.5 = ((bf16[6,128,1152]{2,0,1:T(8,128)(2,1)}), bf16[6,128,1152]{2,0,1:T(8,128)(2,1)}, u32[]{:S(2)}, u32[]{:S(2)}) async-start(bf16[6,128,1152]{2,0,1:T(8,128)(2,1)} %copy.94), calls=%async_computation.5 | async-start | bytes 4718592 | tf_op jit(solution)/shard_map/all_to_all | solution.py:69
  303.4 31.0 %copy-start.5 = (s32[96]{0:T(128)S(1)}, s32[96]{0:T(128)}, u32[]{:S(2)}) copy-start(s32[96]{0:T(128)} %param.8) | copy-start | bytes 1156
  329.5 35.0 %all-to-all-start.4 = ((bf16[6,128,1152]{2,0,1:T(8,128)(2,1)}), bf16[6,128,1152]{2,0,1:T(8,128)(2,1)}, u32[]{:S(2)}, u32[]{:S(2)}) async-start(bf16[6,128,1152]{2,0,1:T(8,128)(2,1)} %copy.93), calls=%async_computation.4 | async-start | bytes 4718592 | tf_op jit(solution)/shard_map/all_to_all | solution.py:71
  382.2 1.9 copy-start.4
  392.8 25.6 %copy-start.3 = (bf16[6,128,1152]{2,1,0:T(8,128)(2,1)S(1)}, bf16[6,128,1152]{2,1,0:T(8,128)(2,1)}, u32[]{:S(2)}) copy-start(bf16[6,128,1152]{2,1,0:T(8,128)(2,1)} %copy-done.2) | copy-start | bytes 5308420
where the time goes:
time: 432 us; the launch traced here: 424 us
  waiting for transfers between devices  130 us (30%)
  local copies, waits for them, and re-layouts  119 us (28%)
  matrix products  82.9 us (19%)
  blocking collectives  53.8 us (12%)
  starting transfers between devices  31.1 us (7%)
  other arithmetic  7.51 us (2%)
    unnamed x24, local copies, waits for them, and re-layouts  41.2 us
    all_to_all x1, waiting for transfers between devices, body(): lax.all_to_all(k_own, 'frame', split_axis=1, concat_axis=0, tiled=True)  29.2 us
    all_to_all x1, blocking collectives, body(): lax.all_to_all(mixed, 'inframe', split_axis=1, concat_axis=2, tiled=True)  28.2 us
    all_to_all x1, waiting for transfers between devices, body(): lax.all_to_all(q_own, 'frame', split_axis=1, concat_axis=0, tiled=True)  26.2 us
    all_to_all x1, waiting for transfers between devices, body(): lax.all_to_all(values, 'inframe', split_axis=2, concat_axis=1, tiled=True)  25.8 us
    all_to_all x1, waiting for transfers between devices, body(): lax.all_to_all(query, 'inframe', split_axis=2, concat_axis=1, tiled=True)  25.8 us
    all_to_all x1, blocking collectives, body(): lax.all_to_all(mixed_two, 'frame', split_axis=0, concat_axis=1, tiled=True)  25.6 us
    sub x1, matrix products, softmax_last(): powers = jnp.exp(scores - top)  23.8 us
  transfers between devices with their start and end apart: 6, of which 6 were waited for; matrix products, arithmetic and copies ran while one was open for 13% of the time, Pallas kernels for 0%

commit v1 on v0

v1 whole, which is shorter than its diff:
```python
import functools
import math

import jax
import jax.numpy as jnp
from jax import lax
from jax.experimental import pallas as pl
from jax.experimental.pallas import tpu as pltpu
from jax.sharding import PartitionSpec as P

MESH = pl.DeviceIdType.MESH
F32, BF16 = jnp.float32, jnp.bfloat16
HEADS = 16
HD = 72
D = HEADS * HD
WIN = 256
LOG2E = 1.0 / math.log(2.0)
NEG = -1e30


def normed(x, shift, scale):
    center = x - jnp.mean(x, axis=-1, keepdims=True)
    spread = jnp.mean(center * center, axis=-1, keepdims=True)
    return (center * lax.rsqrt(spread + 1e-06) * (1.0 + scale) + shift).astype(BF16)


def dot(a, b):
    return jnp.dot(a, b, preferred_element_type=F32)


def dot_t(a, b):
    return lax.dot_general(a, b, (((1,), (1,)), ((), ())), preferred_element_type=F32)


def kernel(
    tokens, clips, mod, wsq, wso, wtq, wto,
    final,
    xin, wq, wo, wo2, q_s, kt_s, v_s, mixed, first_out, recv_t, f32_t, rows_t, qkv_t, mixed_t, out_t,
    mods_t,
    send_a, recv_a, send_b, recv_b, send_c, recv_c, w_sem, all_in,
):
    i = lax.axis_index("frame")
    j = lax.axis_index("inframe")
    x, z = i // 4, i % 4
    y = j // 2
    parity = (x + z) % 2

    def owner_of(l):
        return l + (1 - parity) * ((l + 1) // 4) + parity * ((l + 2) // 3)

    own = jnp.where(parity == 0, j - j // 4, j - (j + 2) // 4)
    idle = jnp.where(parity == 0, j % 4 == 3, j % 4 == 1)
    owner = jnp.logical_not(idle)
    frame = i * 6 + own

    def weight_copy(src, dst, n):
        return pltpu.make_async_copy(src, dst, w_sem.at[n])

    barrier = pltpu.get_barrier_semaphore()

    @pl.loop(1, 8)
    def _(k):
        pl.semaphore_signal(barrier, inc=1, device_id=(i, (j + k) % 8), device_id_type=MESH)

    @pl.loop(1, 16)
    def _(k):
        pl.semaphore_signal(barrier, inc=1, device_id=((i + k) % 16, j), device_id_type=MESH)

    weight_copy(wsq, wq, 0).start()
    weight_copy(wso, wo, 1).start()
    weight_copy(wto, wo2, 2).start()
    pl.semaphore_wait(barrier, 22)

    def token_copy(l, dest):
        return pltpu.make_async_remote_copy(
            src_ref=tokens.at[l], dst_ref=xin.at[j], send_sem=send_a, recv_sem=recv_a.at[j],
            device_id=(i, dest), device_id_type=MESH,
        )

    @pl.loop(0, 6)
    def _(l):
        dest = owner_of(l)

        @pl.when(dest != j)
        def _():
            token_copy(l, dest).start()

    @pl.when(owner)
    def _():
        pltpu.make_async_copy(tokens.at[own], xin.at[j], recv_a.at[j]).start()

    @pl.loop(1, 8)
    def _(k):
        pl.semaphore_signal(all_in, inc=1, device_id=(i, (j + k) % 8), device_id_type=MESH)

    clip_row = clips[...]
    row_id = lax.broadcasted_iota(jnp.int32, (96, 96), 0)
    col_id = lax.broadcasted_iota(jnp.int32, (96, 96), 1)
    clip_rows = jnp.broadcast_to(clip_row, (96, 96))
    clip_col = jnp.sum(jnp.where(row_id == col_id, clip_rows, 0), axis=1, keepdims=True)

    @pl.loop(0, 3)
    def _(n):
        picked = jnp.zeros((96, D), F32)
        for c in range(4):
            picked = jnp.where(clip_col == c, mod[c, pl.ds(3 + n, 1), :], picked)
        mods_t[n] = picked

    weight_copy(wsq, wq, 0).wait()
    weight_copy(wso, wo, 1).wait()
    weight_copy(wto, wo2, 2).wait()

    @pl.when(owner)
    def _():
        lane96 = lax.broadcasted_iota(jnp.int32, (1, 96), 1)
        own_clip = jnp.sum(jnp.where(lane96 == frame, clip_row, 0), axis=1, keepdims=True)

        def own_mod(n):
            picked = jnp.zeros((1, D), F32)
            for c in range(4):
                picked = jnp.where(own_clip == c, mod[c, n : n + 1, :], picked)
            return picked

        shift, scale = own_mod(0), own_mod(1)

        @pl.loop(0, 4)
        def _(s):
            yy = (y + (s + 1) // 2 * (1 - s % 2 * 2) + 4) % 4
            for c in range(2):
                pltpu.make_async_copy(tokens.at[0], xin.at[yy * 2 + c], recv_a.at[yy * 2 + c]).wait()
            rows = xin[pl.ds(2 * yy, 2)].astype(F32).reshape(256, D)
            hidden = normed(rows, shift, scale)
            q = dot(hidden, wq[:, :D]) * (LOG2E * HD**-0.5)
            q_s[pl.ds(2 * yy, 2)] = q.astype(BF16).reshape(2, 128, D)
            k = dot(hidden, wq[:, D : 2 * D])
            kt_s[:, pl.ds(pl.multiple_of(yy * 256, 256), 256)] = k.T.astype(BF16)
            v = dot(hidden, wq[:, 2 * D :])
            v_s[pl.ds(pl.multiple_of(yy * 256, 256), 256), :] = v.astype(BF16)

    weight_copy(wtq, wq, 3).start()
    pl.semaphore_wait(all_in, 7)

    @pl.when(owner)
    def _():
        lane96 = lax.broadcasted_iota(jnp.int32, (1, 96), 1)
        own_clip = jnp.sum(jnp.where(lane96 == frame, clip_row, 0), axis=1, keepdims=True)
        gate = jnp.zeros((1, D), F32)
        for c in range(4):
            gate = jnp.where(own_clip == c, mod[c, 2:3, :], gate)

        @pl.loop(0, 4)
        def _(s):
            t = (x + 2 + 3 * s) % 4
            rows = pl.ds(pl.multiple_of(t * 32, 32), 32)

            def head(h):
                at = jnp.minimum(h * HD // 128, 7)
                off = pl.multiple_of(at * 128, 128)
                lane = lax.broadcasted_iota(jnp.int32, (1, WIN), 1) + (at * 128 - h * HD)
                inside = jnp.logical_and(lane >= 0, lane < HD)
                q = q_s[:, rows, pl.ds(off, WIN)].reshape(256, WIN)
                q = jnp.where(inside, q, jnp.zeros_like(q))
                scores = dot(q, kt_s[pl.ds(off, WIN), :])
                powers = jnp.exp2(scores - jnp.max(scores, axis=-1, keepdims=True))
                total = jnp.sum(powers, axis=-1, keepdims=True)
                out = dot(powers.astype(BF16), v_s[:, pl.ds(off, WIN)]) / total
                mixed[:, pl.ds(off, WIN)] = jnp.where(inside, out, mixed[:, pl.ds(off, WIN)])

            @pl.loop(0, HEADS // 2)
            def _(u):
                head(2 * u)
                head(2 * u + 1)

            proj = dot(mixed[...].astype(BF16), wo[...])
            base = xin[:, rows, :].astype(F32).reshape(256, D)
            first = base + gate * proj
            first_out[:, pl.ds(t * 4, 4)] = first.reshape(8, 4, 8, D).astype(BF16)

            @pl.loop(0, 32)
            def _(n):
                dj, di = n // 4, t * 4 + n % 4

                @pl.when(jnp.logical_or(dj != j, di != i))
                def _():
                    pltpu.make_async_remote_copy(
                        src_ref=first_out.at[dj, di], dst_ref=recv_t.at[frame], send_sem=send_b,
                        recv_sem=recv_b, device_id=(di, dj), device_id_type=MESH,
                    ).start()

        pltpu.make_async_copy(first_out.at[j, i], recv_t.at[frame], recv_b).start()

    weight_copy(wtq, wq, 3).wait()
    pltpu.make_async_copy(recv_t, recv_t, recv_b).wait()

    @pl.loop(0, 12)
    def _(c):
        rows = recv_t[pl.ds(c * 8, 8)].astype(F32).reshape(64, D)
        for b in range(9):
            f32_t[b, pl.ds(pl.multiple_of(c * 64, 64), 64), :] = rows[:, b * 128 : b * 128 + 128]

    @pl.loop(0, 8)
    def _(p):
        rows = jnp.concatenate([f32_t[b, pl.ds(p, 96, stride=8), :] for b in range(9)], axis=1)
        rows_t[pl.ds(pl.multiple_of(p * 96, 96), 96), :] = normed(rows, mods_t[0], mods_t[1])

    @pl.loop(0, 3)
    def _(c):
        at = pl.ds(pl.multiple_of(c * 256, 256), 256)
        hidden = rows_t[at, :]
        q = dot(hidden, wq[:, :D]) * (LOG2E * HD**-0.5)
        qkv_t[at, :D] = q.astype(BF16)
        qkv_t[at, D : 2 * D] = dot(hidden, wq[:, D : 2 * D]).astype(BF16)
        qkv_t[at, 2 * D :] = dot(hidden, wq[:, 2 * D :]).astype(BF16)

    same = clip_col == clip_rows

    @pl.loop(0, 8)
    def _(p):
        at = pl.ds(pl.multiple_of(p * 96, 96), 96)
        for h in range(HEADS):
            off = min(h * HD // 128, 7) * 128
            lane = lax.broadcasted_iota(jnp.int32, (1, WIN), 1) + (off - h * HD)
            inside = jnp.logical_and(lane >= 0, lane < HD)
            q = qkv_t[at, off : off + WIN]
            q = jnp.where(inside, q, jnp.zeros_like(q))
            scores = dot_t(q, qkv_t[at, D + off : D + off + WIN])
            scores = jnp.where(same, scores, NEG)
            powers = jnp.exp2(scores - jnp.max(scores, axis=-1, keepdims=True))
            total = jnp.sum(powers, axis=-1, keepdims=True)
            out = dot(powers.astype(BF16), qkv_t[at, 2 * D + off : 2 * D + off + WIN]) / total
            mixed_t[at, off : off + WIN] = jnp.where(inside, out, mixed_t[at, off : off + WIN])

    @pl.loop(0, 4)
    def _(c):
        proj = dot(mixed_t[pl.ds(pl.multiple_of(c * 192, 192), 192), :].astype(BF16), wo2[...])
        for n in range(2):
            at = pl.ds(c * 2 + n, 96, stride=8)
            for b in range(9):
                cols = slice(b * 128, b * 128 + 128)
                f32_t[b, at, :] = f32_t[b, at, :] + mods_t[2, :, cols] * proj[n * 96 : n * 96 + 96, cols]

    @pl.loop(0, 12)
    def _(c):
        at = pl.ds(pl.multiple_of(c * 64, 64), 64)
        rows = jnp.concatenate([f32_t[b, at, :] for b in range(9)], axis=1)
        out_t[pl.ds(c * 8, 8)] = rows.reshape(8, 8, D).astype(BF16)

    @pl.loop(1, 16)
    def _(k):
        di = (i + k) % 16
        pltpu.make_async_remote_copy(
            src_ref=out_t.at[pl.ds(di * 6, 6)], dst_ref=final.at[i], send_sem=send_c,
            recv_sem=recv_c, device_id=(di, j), device_id_type=MESH,
        ).start()

    pltpu.make_async_copy(out_t.at[pl.ds(i * 6, 6)], final.at[i], recv_c).start()

    @pl.loop(0, 6)
    def _(l):
        dest = owner_of(l)

        @pl.when(dest != j)
        def _():
            token_copy(l, dest).wait_send()

    @pl.when(owner)
    def _():
        @pl.loop(0, 127)
        def _(n):
            pltpu.make_async_copy(first_out.at[0, 0], recv_t.at[0], send_b).wait()

    @pl.loop(0, 15)
    def _(n):
        pltpu.make_async_copy(out_t.at[pl.ds(0, 6)], out_t.at[pl.ds(0, 6)], send_c).wait()

    pltpu.make_async_copy(final, final, recv_c).wait()


def body(tokens, clip_ids, modulation, w_spatial_qkv, w_spatial_out, w_temporal_qkv, w_temporal_out):
    any_, vmem = pl.BlockSpec(memory_space=pl.ANY), pl.BlockSpec(memory_space=pltpu.VMEM)
    dma = pltpu.SemaphoreType.DMA
    final = pl.pallas_call(
        kernel,
        out_shape=jax.ShapeDtypeStruct((16, 6, 8, D), BF16),
        in_specs=[any_, vmem, vmem, any_, any_, any_, any_],
        out_specs=any_,
        scratch_shapes=[
            pltpu.VMEM((8, 128, D), BF16),
            pltpu.VMEM((D, 3 * D), BF16),
            pltpu.VMEM((D, D), BF16),
            pltpu.VMEM((D, D), BF16),
            pltpu.VMEM((8, 128, D), BF16),
            pltpu.VMEM((D, 1024), BF16),
            pltpu.VMEM((1024, D), BF16),
            pltpu.VMEM((256, D), F32),
            pltpu.VMEM((8, 16, 8, D), BF16),
            pltpu.VMEM((96, 8, D), BF16),
            pltpu.VMEM((9, 768, 128), F32),
            pltpu.VMEM((768, D), BF16),
            pltpu.VMEM((768, 3 * D), BF16),
            pltpu.VMEM((768, D), F32),
            pltpu.VMEM((96, 8, D), BF16),
            pltpu.VMEM((3, 96, D), F32),
            dma, dma((8,)), dma, dma, dma, dma, dma((4,)),
            pltpu.SemaphoreType.REGULAR,
        ],
        compiler_params=pltpu.CompilerParams(
            collective_id=0, has_side_effects=True, vmem_limit_bytes=60 * 1024 * 1024
        ),
        name="block",
    )(tokens, clip_ids.reshape(1, 96), modulation, w_spatial_qkv, w_spatial_out, w_temporal_qkv, w_temporal_out)
    return final.transpose(1, 0, 2, 3).reshape(6, 128, D)


def solution(mesh):
    in_specs = (P("frame", "inframe", None), P(), P(), P(), P(), P(), P())
    out_specs = P("frame", "inframe", None)
    return jax.shard_map(body, mesh=mesh, in_specs=in_specs, out_specs=out_specs, check_vma=False)
```

time: 432 us -> 166 us (0.38)
  the two profiles are of different devices: /device:TPU:0 before, /device:TPU:125 now
where the time goes in v1:
time: 166 us
  Pallas kernels  161 us (97%)
  local copies, waits for them, and re-layouts  4.46 us (3%)
    pallas_call x1, Pallas kernels, body(): pl.pallas_call(kernel, out_shape=jax.ShapeDtypeStruct((16, 6, 8, D), BF16...  161 us

profile of v1, /device:TPU:125, one launch (start us, length us, event | category | flops | bytes accessed | tf_op | source)
XLA Modules:
  0.0 165.6 jit_solution(15168768591942207031)
XLA Ops:
  0.0 1.6 copy.9.mod
  1.6 161.2 %block.1 = bf16[16,6,8,1152]{3,2,1,0:T(8,128)(2,1)} custom-call(bf16[6,128,1152]{2,1,0:T(8,128)(2,1)} %tokens.1, s32[1,96]{1,0:T(1,128)} %bitcast.6, f32[4,6,1152]{2,1,0:T(8,128)} %copy.9.mod, bf16[1152,3456]{1,0:T(8,128)(2,1)} %wsq.1, bf16[1152,1152]{1,0:T(8,128)(2,1)} %wso.1, bf16[1152,3456]{1,0:T(8,128)(2,1)} %wtq.1, bf16[1152,1152]{1,0:T(8,128)(2,1)} %wto.1), custom_call_target="tpu_custom_call" | custom-call | tf_op jit(solution)/shard_map/block/pallas_call | solution.py:282
  162.8 2.9 %copy_bitcast_fusion = bf16[6,128,1152]{2,1,0:T(8,128)(2,1)} fusion(bf16[16,6,8,1152]{3,2,1,0:T(8,128)(2,1)} %block.1), kind=kLoop, calls=%fused_computation | loop fusion | bytes 3538944 | tf_op jit(solution)/shard_map/reshape | solution.py:312

commit v2 on v1

v2 whole, which is shorter than its diff:
```python
import math

import jax
import jax.numpy as jnp
from jax import lax
from jax.experimental import pallas as pl
from jax.experimental.pallas import tpu as pltpu
from jax.sharding import PartitionSpec as P

MESH = pl.DeviceIdType.MESH
F32, BF16 = jnp.float32, jnp.bfloat16
HEADS = 16
HD = 72
D = HEADS * HD
WIN = 256
Q_SCALE = HD**-0.5 / math.log(2.0)
NEG = -1e30


def hops(*offsets):
    return sum(min(o, 4 - o) for o in offsets)


YZ_FAR_FIRST = sorted(((dy, dz) for dy in range(4) for dz in range(4)), key=lambda o: -hops(*o))


def normed(x, shift, scale):
    center = x - jnp.mean(x, axis=-1, keepdims=True)
    spread = jnp.mean(center * center, axis=-1, keepdims=True)
    return (center * lax.rsqrt(spread + 1e-06) * (1.0 + scale) + shift).astype(BF16)


def dot(a, b):
    return jnp.dot(a, b, preferred_element_type=F32)


def dot_t(a, b):
    return lax.dot_general(a, b, (((1,), (1,)), ((), ())), preferred_element_type=F32)


def window(h):
    return min(h * HD // 128, 7) * 128


def kernel(
    tokens, clips, mod, wsq, wso, wtq, wto,
    final,
    xin, wq, wo, wo2, qt_s, k_s, vt_s, score, power, mixt, first_out, recv_t, f32_t, rows_t, qkv_t, out_t, mods_t,
    send_a, recv_a, send_b, recv_b, send_c, recv_c, w_sem, all_in,
):
    i = lax.axis_index("frame")
    j = lax.axis_index("inframe")
    x, z = i // 4, i % 4
    y, core = j // 2, j % 2
    parity = (x + z) % 2

    def owned(dev):
        return jnp.where(parity == 0, dev - dev // 4, dev - (dev + 2) // 4)

    def owns(dev):
        return jnp.where(parity == 0, dev % 4 != 3, dev % 4 != 1)

    own, owner = owned(j), owns(j)
    frame = i * 6 + own

    def weight_copy(src, dst, n):
        return pltpu.make_async_copy(src, dst, w_sem.at[n])

    barrier = pltpu.get_barrier_semaphore()

    @pl.loop(1, 8)
    def _(k):
        pl.semaphore_signal(barrier, inc=1, device_id=(i, (j + k) % 8), device_id_type=MESH)

    @pl.loop(1, 16)
    def _(k):
        pl.semaphore_signal(barrier, inc=1, device_id=((i + k) % 16, j), device_id_type=MESH)

    weight_copy(wsq, wq, 0).start()
    weight_copy(wso, wo, 1).start()
    weight_copy(wto, wo2, 2).start()
    pl.semaphore_wait(barrier, 22)

    def token_copy(dest):
        return pltpu.make_async_remote_copy(
            src_ref=tokens.at[owned(dest)], dst_ref=xin.at[j], send_sem=send_a, recv_sem=recv_a.at[j],
            device_id=(i, dest), device_id_type=MESH,
        )

    others = [(dy, dc) for dy in (2, 1, 3, 0) for dc in (0, 1) if (dy, dc) != (0, 0)]
    for dy, dc in others:
        dest = (y + dy) % 4 * 2 + (core + dc) % 2

        @pl.when(owns(dest))
        def _(dest=dest):
            token_copy(dest).start()

    @pl.when(owner)
    def _():
        pltpu.make_async_copy(tokens.at[own], xin.at[j], recv_a.at[j]).start()

    @pl.loop(1, 8)
    def _(k):
        pl.semaphore_signal(all_in, inc=1, device_id=(i, (j + k) % 8), device_id_type=MESH)

    def frame_at(slot):
        step = slot // 48 + 1 + slot % 48 // 24 * 2
        return (x + 4 - step % 4) % 4 * 24 + slot % 24

    clip_row = clips[...]
    row_id = lax.broadcasted_iota(jnp.int32, (96, 96), 0)
    col_id = lax.broadcasted_iota(jnp.int32, (96, 96), 1)
    clip_rows = jnp.broadcast_to(clip_row, (96, 96))
    clip_natural = jnp.sum(jnp.where(row_id == col_id, clip_rows, 0), axis=1, keepdims=True)
    clip_col = jnp.sum(jnp.where(frame_at(row_id) == col_id, clip_rows, 0), axis=1, keepdims=True)
    clip_slots = jnp.sum(jnp.where(row_id == frame_at(col_id), clip_natural, 0), axis=0, keepdims=True)

    @pl.loop(0, 3)
    def _(n):
        picked = jnp.zeros((96, D), F32)
        for c in range(4):
            picked = jnp.where(clip_col == c, mod[3 + n, c : c + 1, :], picked)
        mods_t[n] = picked

    lane96 = lax.broadcasted_iota(jnp.int32, (1, 96), 1)
    own_clip = jnp.sum(jnp.where(lane96 == frame, clip_row, 0), axis=1, keepdims=True)

    def own_mod(n):
        picked = jnp.zeros((1, D), F32)
        for c in range(4):
            picked = jnp.where(own_clip == c, mod[n, c : c + 1, :], picked)
        return picked

    vt_s[:, HD:, :] = jnp.ones((HEADS, 8, 1024), BF16)

    weight_copy(wsq, wq, 0).wait()
    weight_copy(wso, wo, 1).wait()
    weight_copy(wto, wo2, 2).wait()

    @pl.when(owner)
    def _():
        shift, scale = own_mod(0), own_mod(1)

        @pl.loop(0, 4)
        def _(s):
            yy = (y + jnp.where(s == 0, 0, jnp.where(s == 1, 2, jnp.where(s == 2, 1, 3)))) % 4
            for c in range(2):
                pltpu.make_async_copy(tokens.at[0], xin.at[yy * 2 + c], recv_a.at[yy * 2 + c]).wait()
            rows = xin[pl.ds(2 * yy, 2)].astype(F32).reshape(256, D)
            hidden = normed(rows, shift, scale)
            at = pl.ds(pl.multiple_of(yy * 256, 256), 256)
            q = (dot(hidden, wq[:, :D]) * Q_SCALE).reshape(2, 2, 2, 32, D)
            for par in range(2):
                qt = q[:, :, par].reshape(128, D).T
                cols = pl.ds(pl.multiple_of(par * 512 + yy * 128, 128), 128)
                for h in range(HEADS):
                    off = window(h)
                    row = lax.broadcasted_iota(jnp.int32, (WIN, 1), 0) + (off - h * HD)
                    inside = jnp.logical_and(row >= 0, row < HD)
                    qt_s[h, :, cols] = jnp.where(inside, qt[off : off + WIN], 0.0).astype(BF16)
            k_s[at, :] = dot(hidden, wq[:, D : 2 * D]).astype(BF16)
            v = dot(hidden, wq[:, 2 * D :])
            vt_s[:, :HD, at] = v.T.reshape(HEADS, HD, 256).astype(BF16)

    weight_copy(wtq, wq, 3).start()
    pl.semaphore_wait(all_in, 7)

    @pl.when(owner)
    def _():
        gate = own_mod(2)

        @pl.loop(0, 2)
        def _(s):
            par = (x + 1 + s) % 2
            cols = pl.ds(pl.multiple_of(par * 512, 512), 512)

            def scores(h, n):
                off = pl.multiple_of(jnp.minimum(h * HD // 128, 7) * 128, 128)
                score[n] = dot(k_s[:, pl.ds(off, WIN)], qt_s[h, :, cols])

            def attend(h, n):
                values = score[n]
                top = jnp.max(values, axis=0, keepdims=True)
                power[n] = jnp.exp2(values - top).astype(BF16)
                out = dot(vt_s[h], power[n])
                mixt[pl.ds(pl.multiple_of(h * HD, 8), HD), :] = out[:HD] * (1.0 / out[HD : HD + 1])

            scores(0, 0)

            @pl.loop(0, HEADS // 2)
            def _(u):
                scores(2 * u + 1, 1)
                attend(2 * u, 0)
                scores(jnp.minimum(2 * u + 2, HEADS - 1), 0)
                attend(2 * u + 1, 1)

            @pl.loop(0, 2)
            def _(b):
                mixed = mixt[:, pl.ds(pl.multiple_of(b * 256, 256), 256)].T.astype(BF16)
                proj = dot(mixed, wo[...]).reshape(4, 2, 32, D)
                devs = pl.ds(4 * b, 4)
                for a in range(2):
                    at = pl.ds(pl.multiple_of(a * 64 + par * 32, 32), 32)
                    first = xin[devs, at, :].astype(F32) + gate * proj[:, a]
                    first_out[devs, pl.ds(8 * a + 4 * par, 4)] = first.reshape(4, 4, 8, D).astype(BF16)

            for dy, dz in YZ_FAR_FIRST:
                for dc in range(2):
                    for k in range(2):
                        dx = (1 + s + 2 * k) % 4
                        di = (x + dx) % 4 * 4 + (z + dz) % 4
                        dj = (y + dy) % 4 * 2 + (core + dc) % 2
                        slot = (s * 2 + k) * 24 + z * 6 + own
                        copy = pltpu.make_async_remote_copy(
                            src_ref=first_out.at[dj, di], dst_ref=recv_t.at[slot], send_sem=send_b,
                            recv_sem=recv_b.at[s], device_id=(di, dj), device_id_type=MESH,
                        )
                        if (dy, dz, dc, k) != (0, 0, 0, 1):
                            copy.start()
                        else:
                            pl.when(s == 0)(copy.start)

        pltpu.make_async_copy(first_out.at[j, i], recv_t.at[72 + z * 6 + own], recv_b.at[1]).start()

    weight_copy(wtq, wq, 3).wait()

    @pl.loop(0, 2)
    def _(s):
        slots = recv_t.at[pl.ds(48 * s, 48)]
        pltpu.make_async_copy(slots, slots, recv_b.at[s]).wait()

        @pl.loop(0, 6)
        def _(c):
            rows = recv_t[pl.ds(48 * s + c * 8, 8)].astype(F32).reshape(64, D)
            for b in range(9):
                f32_t[b, pl.ds(pl.multiple_of(s * 384 + c * 64, 64), 64), :] = rows[:, b * 128 : b * 128 + 128]

        half = pl.ds(pl.multiple_of(48 * s, 48), 48)

        @pl.loop(0, 8)
        def _(p):
            rows = jnp.concatenate([f32_t[b, pl.ds(s * 384 + p, 48, stride=8), :] for b in range(9)], axis=1)
            at = pl.ds(pl.multiple_of(p * 48, 48), 48)
            rows_t[s, at, :] = normed(rows, mods_t[0, half, :], mods_t[1, half, :])

        hidden = rows_t[s]
        qkv_t[s, :, :D] = (dot(hidden, wq[:, :D]) * Q_SCALE).astype(BF16)
        qkv_t[s, :, D : 2 * D] = dot(hidden, wq[:, D : 2 * D]).astype(BF16)
        qkv_t[s, :, 2 * D :] = dot(hidden, wq[:, 2 * D :]).astype(BF16)

    same = clip_col == clip_slots

    @pl.loop(0, 8)
    def _(p):
        at = pl.ds(pl.multiple_of(p * 48, 48), 48)
        blocks = [jnp.zeros((96, 128), F32) for _ in range(9)]
        for h in range(HEADS):
            off = window(h)
            lane = lax.broadcasted_iota(jnp.int32, (1, WIN), 1) + (off - h * HD)
            inside = jnp.logical_and(lane >= 0, lane < HD)

            def part(n):
                cols = slice(n * D + off, n * D + off + WIN)
                return jnp.concatenate([qkv_t[0, at, cols], qkv_t[1, at, cols]], axis=0)

            q = part(0)
            q = jnp.where(inside, q, jnp.zeros_like(q))
            scores = jnp.where(same, dot_t(q, part(1)), NEG)
            powers = jnp.exp2(scores - jnp.max(scores, axis=-1, keepdims=True))
            total = jnp.sum(powers, axis=-1, keepdims=True)
            out = dot(powers.astype(BF16), part(2)) * (1.0 / total)
            for b in range(off // 128, off // 128 + 2):
                lanes = slice(b * 128 - off, b * 128 - off + 128)
                blocks[b] = jnp.where(inside[:, lanes], out[:, lanes], blocks[b])
        for b in range(9):
            cols = slice(b * 128, b * 128 + 128)
            rows_t[0, at, cols] = blocks[b][:48].astype(BF16)
            rows_t[1, at, cols] = blocks[b][48:].astype(BF16)

    def back_copy(s, k, dz):
        dx = (4 - (1 + s + 2 * k)) % 4
        di = (x + dx) % 4 * 4 + (z + dz) % 4
        slot = (s * 2 + k) * 24 + (z + dz) % 4 * 6
        return di, out_t.at[pl.ds(slot, 6)]

    for s in range(2):
        proj = dot(rows_t[s], wo2[...])
        for p in range(8):
            at = pl.ds(s * 384 + p, 48, stride=8)
            for b in range(9):
                cols = slice(b * 128, b * 128 + 128)
                f32_t[b, at, :] = f32_t[b, at, :] + mods_t[2, s * 48 : s * 48 + 48, cols] * proj[p * 48 : p * 48 + 48, cols]

        @pl.loop(0, 6)
        def _(c, s=s):
            at = pl.ds(pl.multiple_of(s * 384 + c * 64, 64), 64)
            rows = jnp.concatenate([f32_t[b, at, :] for b in range(9)], axis=1)
            out_t[pl.ds(s * 48 + c * 8, 8)] = rows.reshape(8, 8, D).astype(BF16)

        for dz in (2, 1, 3, 0):
            for k in range(2):
                di, src = back_copy(s, k, dz)
                if (s, k, dz) == (1, 1, 0):
                    pltpu.make_async_copy(src, final.at[:, i], recv_c).start()
                else:
                    pltpu.make_async_remote_copy(
                        src_ref=src, dst_ref=final.at[:, i], send_sem=send_c, recv_sem=recv_c,
                        device_id=(di, j), device_id_type=MESH,
                    ).start()

    for dy, dc in others:
        dest = (y + dy) % 4 * 2 + (core + dc) % 2

        @pl.when(owns(dest))
        def _(dest=dest):
            token_copy(dest).wait_send()

    @pl.when(owner)
    def _():
        @pl.loop(0, 127)
        def _(n):
            pltpu.make_async_copy(first_out.at[0, 0], recv_t.at[0], send_b).wait()

    @pl.loop(0, 15)
    def _(n):
        pltpu.make_async_copy(out_t.at[pl.ds(0, 6)], out_t.at[pl.ds(0, 6)], send_c).wait()

    pltpu.make_async_copy(final, final, recv_c).wait()


def body(tokens, clip_ids, modulation, w_spatial_qkv, w_spatial_out, w_temporal_qkv, w_temporal_out):
    any_, vmem = pl.BlockSpec(memory_space=pl.ANY), pl.BlockSpec(memory_space=pltpu.VMEM)
    dma = pltpu.SemaphoreType.DMA
    final = pl.pallas_call(
        kernel,
        out_shape=jax.ShapeDtypeStruct((6, 16, 8, D), BF16),
        in_specs=[any_, vmem, vmem, any_, any_, any_, any_],
        out_specs=any_,
        scratch_shapes=[
            pltpu.VMEM((8, 128, D), BF16),
            pltpu.VMEM((D, 3 * D), BF16),
            pltpu.VMEM((D, D), BF16),
            pltpu.VMEM((D, D), BF16),
            pltpu.VMEM((HEADS, WIN, 1024), BF16),
            pltpu.VMEM((1024, D), BF16),
            pltpu.VMEM((HEADS, HD + 8, 1024), BF16),
            pltpu.VMEM((2, 1024, 512), F32),
            pltpu.VMEM((2, 1024, 512), BF16),
            pltpu.VMEM((D, 512), F32),
            pltpu.VMEM((8, 16, 8, D), BF16),
            pltpu.VMEM((96, 8, D), BF16),
            pltpu.VMEM((9, 768, 128), F32),
            pltpu.VMEM((2, 384, D), BF16),
            pltpu.VMEM((2, 384, 3 * D), BF16),
            pltpu.VMEM((96, 8, D), BF16),
            pltpu.VMEM((3, 96, D), F32),
            dma, dma((8,)), dma, dma((2,)), dma, dma, dma((4,)),
            pltpu.SemaphoreType.REGULAR,
        ],
        compiler_params=pltpu.CompilerParams(
            collective_id=0, has_side_effects=True, vmem_limit_bytes=63 * 1024 * 1024
        ),
        name="block",
    )(
        tokens, clip_ids.reshape(1, 96), modulation.transpose(1, 0, 2),
        w_spatial_qkv, w_spatial_out, w_temporal_qkv, w_temporal_out,
    )
    return final.reshape(6, 128, D)


def solution(mesh):
    in_specs = (P("frame", "inframe", None), P(), P(), P(), P(), P(), P())
    out_specs = P("frame", "inframe", None)
    return jax.shard_map(body, mesh=mesh, in_specs=in_specs, out_specs=out_specs, check_vma=False)
```

time: 166 us -> 133 us (0.80)
  the two profiles are of different devices: /device:TPU:125 before, /device:TPU:14 now
where the time goes in v2:
time: 133 us
  Pallas kernels  130 us (98%)
  local copies, waits for them, and re-layouts  2.82 us (2%)
    pallas_call x1, Pallas kernels, body(): pl.pallas_call(kernel, out_shape=jax.ShapeDtypeStruct((6, 16, 8, D), BF16...  130 us
    unnamed x1, local copies, waits for them, and re-layouts  2.82 us

profile of v2, /device:TPU:14, one launch (start us, length us, event | category | flops | bytes accessed | tf_op | source)
XLA Modules:
  0.0 133.3 jit_solution(6727934792933450692)
XLA Ops:
  0.0 130.5 %block.1 = bf16[6,16,8,1152]{3,2,1,0:T(8,128)(2,1)} custom-call(bf16[6,128,1152]{2,1,0:T(8,128)(2,1)} %tokens.1, s32[1,96]{1,0:T(1,128)} %bitcast.5, f32[6,4,1152]{2,1,0:T(4,128)} %bitcast.4, bf16[1152,3456]{1,0:T(8,128)(2,1)} %wsq.1, bf16[1152,1152]{1,0:T(8,128)(2,1)} %wso.1, bf16[1152,3456]{1,0:T(8,128)(2,1)} %wtq.1, bf16[1152,1152]{1,0:T(8,128)(2,1)} %wto.1), custom_call_target="tpu_custom_call" | custom-call | tf_op jit(solution)/shard_map/block/pallas_call | solution.py:334
  130.5 2.8 %copy.9 = bf16[6,128,1152]{2,1,0:T(8,128)(2,1)} copy(bf16[6,128,1152]{2,1,0:T(8,128)(2,1)} %bitcast.3) | data formatting | bytes 3538944

commit v3 on v2

v3 whole, which is shorter than its diff:
```python
import math

import jax
import jax.numpy as jnp
from jax import lax
from jax.experimental import pallas as pl
from jax.experimental.pallas import tpu as pltpu
from jax.sharding import PartitionSpec as P

MESH = pl.DeviceIdType.MESH
F32, BF16 = jnp.float32, jnp.bfloat16
HEADS = 16
HALF = 8
HD = 72
D = HEADS * HD
WIN = 256
WIDE = 640
Q_SCALE = HD**-0.5 / math.log(2.0)
NEG = -1e30


def hops(*offsets):
    return sum(min(o, 4 - o) for o in offsets)


YZ_FAR_FIRST = sorted(((dy, dz) for dy in range(4) for dz in range(4)), key=lambda o: -hops(*o))
XZ_FAR_FIRST = YZ_FAR_FIRST[:-1]


def normed(x, shift, scale):
    center = x - jnp.mean(x, axis=-1, keepdims=True)
    spread = jnp.mean(center * center, axis=-1, keepdims=True)
    return (center * lax.rsqrt(spread + 1e-06) * (1.0 + scale) + shift).astype(BF16)


def dot(a, b):
    return jnp.dot(a, b, preferred_element_type=F32)


def dot_t(a, b):
    return lax.dot_general(a, b, (((1,), (1,)), ((), ())), preferred_element_type=F32)


def window(h):
    return min(h * HD // 128, 7) * 128


def kernel(
    tokens, clips, mod, wsq, wso, wtq, wto,
    final,
    xin, wq, wo, wo2, qtf, vtf, qt_s, k_s, vt_s, score, power, mixt, mix_out, mix_all, first_out, recv_t, f32_t,
    rows_a, rows_b, qkv_a, qkv_b, out_t, mods_t,
    send_a, recv_a, send_m, recv_m, send_b, recv_b, send_c, recv_c, w_sem, all_in,
):
    i = lax.axis_index("frame")
    j = lax.axis_index("inframe")
    x, z = i // 4, i % 4
    y, core = j // 2, j % 2
    parity = (x + z) % 2
    sibling = y * 2 + 1 - core

    count = 2 - (y + parity) % 2

    def weight_copy(src, dst, n):
        return pltpu.make_async_copy(src, dst, w_sem.at[n])

    barrier = pltpu.get_barrier_semaphore()

    @pl.loop(1, 8)
    def _(k):
        pl.semaphore_signal(barrier, inc=1, device_id=(i, (j + k) % 8), device_id_type=MESH)

    @pl.loop(1, 16)
    def _(k):
        pl.semaphore_signal(barrier, inc=1, device_id=((i + k) % 16, j), device_id_type=MESH)

    weight_copy(wsq, wq, 0).start()
    weight_copy(wso, wo, 1).start()
    weight_copy(wto, wo2, 2).start()
    pl.semaphore_wait(barrier, 22)

    def token_copy(src, f, block, dest):
        return pltpu.make_async_remote_copy(
            src_ref=src, dst_ref=xin.at[f, block], send_sem=send_a, recv_sem=recv_a.at[f, block],
            device_id=(i, dest), device_id_type=MESH,
        )

    for dy in (2, 1, 3):
        token_copy(tokens.at[(y + dy) % 4], 0, j, (y + dy) % 4 * 2 + core).start()
    token_copy(tokens.at[y], 0, j, sibling).start()
    pltpu.make_async_copy(tokens.at[y], xin.at[0, j], recv_a.at[0, j]).start()
    for e in range(2):
        chip = parity + 2 * e

        @pl.when(chip != y)
        def _(e=e, chip=chip):
            token_copy(tokens.at[4 + e], 1, j, chip * 2 + core).start()

        @pl.when(chip == y)
        def _(e=e):
            token_copy(tokens.at[4 + e], 1, j, sibling).start()
            pltpu.make_async_copy(tokens.at[4 + e], xin.at[1, j], recv_a.at[1, j]).start()

    @pl.loop(1, 8)
    def _(k):
        pl.semaphore_signal(all_in, inc=1, device_id=(i, (j + k) % 8), device_id_type=MESH)

    def frame_at(slot):
        late = slot - 64
        return jnp.where(slot < 64, slot // 4 * 6 + slot % 4, late // 2 * 6 + 4 + late % 2)

    clip_row = clips[...]
    row_id = lax.broadcasted_iota(jnp.int32, (96, 96), 0)
    col_id = lax.broadcasted_iota(jnp.int32, (96, 96), 1)
    clip_rows = jnp.broadcast_to(clip_row, (96, 96))
    clip_natural = jnp.sum(jnp.where(row_id == col_id, clip_rows, 0), axis=1, keepdims=True)
    clip_col = jnp.sum(jnp.where(frame_at(row_id) == col_id, clip_rows, 0), axis=1, keepdims=True)
    clip_slots = jnp.sum(jnp.where(row_id == frame_at(col_id), clip_natural, 0), axis=0, keepdims=True)

    @pl.loop(0, 3)
    def _(n):
        picked = jnp.zeros((96, D), F32)
        for c in range(4):
            picked = jnp.where(clip_col == c, mod[3 + n, c : c + 1, :], picked)
        mods_t[n] = picked

    vt_s[:, HD:, :] = jnp.ones((HALF, 8, 1024), BF16)

    weight_copy(wsq, wq, 0).wait()
    weight_copy(wso, wo, 1).wait()
    weight_copy(wto, wo2, 2).wait()

    first_lane = pl.multiple_of(core * 512, 512)

    def place(h):
        low = core * 64 + h * HD
        return low, pl.multiple_of(jnp.minimum(low // 128, 3) * 128, 128)

    @pl.loop(0, 2)
    def _(f):
      @pl.when(f < count)
      def _():
        frame = i * 6 + jnp.where(f == 0, y, 4 + y // 2)
        lane96 = lax.broadcasted_iota(jnp.int32, (1, 96), 1)
        own_clip = jnp.sum(jnp.where(lane96 == frame, clip_row, 0), axis=1, keepdims=True)

        def own_mod(n):
            picked = jnp.zeros((1, D), F32)
            for c in range(4):
                picked = jnp.where(own_clip == c, mod[n, c : c + 1, :], picked)
            return picked

        shift, scale, gate = own_mod(0), own_mod(1), own_mod(2)

        @pl.loop(0, 4)
        def _(s):
            yy = (y + jnp.where(s == 0, 0, jnp.where(s == 1, 2, jnp.where(s == 2, 1, 3)))) % 4

            def arrived(block):
                pltpu.make_async_copy(tokens.at[0], xin.at[f, block], recv_a.at[f, block]).wait()

            arrived(yy * 2 + core)

            @pl.when(s > 0)
            def _():
                token_copy(xin.at[f, yy * 2 + core], f, yy * 2 + core, sibling).start()

            arrived(yy * 2 + 1 - core)
            rows = xin[f, pl.ds(2 * yy, 2)].astype(F32).reshape(256, D)
            hidden = normed(rows, shift, scale)
            at = pl.ds(pl.multiple_of(yy * 256, 256), 256)

            def project(n):
                return dot(hidden, wq[:, pl.ds(pl.multiple_of(n * D + first_lane, 128), WIDE)])

            q = (project(0) * Q_SCALE).reshape(2, 2, 2, 32, WIDE)
            for par in range(2):
                qtf[...] = q[:, :, par].reshape(128, WIDE).T
                cols = pl.ds(pl.multiple_of(par * 512 + yy * 128, 128), 128)
                for h in range(HALF):
                    low, off = place(h)
                    row = lax.broadcasted_iota(jnp.int32, (WIN, 1), 0) + (off - low)
                    inside = jnp.logical_and(row >= 0, row < HD)
                    qt_s[h, :, cols] = jnp.where(inside, qtf[pl.ds(off, WIN), :], 0.0).astype(BF16)
            k_s[at, :] = project(1).astype(BF16)
            vtf[...] = project(2).T
            for h in range(HALF):
                low, _ = place(h)
                vt_s[h, :HD, at] = vtf[pl.ds(pl.multiple_of(low, 8), HD), :].astype(BF16)

        @pl.when(f == count - 1)
        def _():
            weight_copy(wtq, wq, 3).start()

        @pl.loop(0, 2)
        def _(n):
            par = (x + n - core + 2) % 2
            cols = pl.ds(pl.multiple_of(par * 512, 512), 512)

            def scores(h, buf):
                _, off = place(h)
                score[buf] = dot(k_s[:, pl.ds(off, WIN)], qt_s[h, :, cols])

            def attend(h, buf):
                values = score[buf]
                top = jnp.max(values, axis=0, keepdims=True)
                power[buf] = jnp.exp2(values - top).astype(BF16)
                out = dot(vt_s[h], power[buf])
                mixt[pl.ds(pl.multiple_of(h * HD, 8), HD), :] = out[:HD] * (1.0 / out[HD : HD + 1])

            scores(0, 0)

            @pl.loop(0, HALF // 2)
            def _(u):
                scores(2 * u + 1, 1)
                attend(2 * u, 0)
                scores(jnp.minimum(2 * u + 2, HALF - 1), 0)
                attend(2 * u + 1, 1)

            own_rows = pl.ds(pl.multiple_of(core * HALF * HD, HALF * HD), HALF * HD)

            @pl.when(n == 0)
            def _():
                mix_out[f] = mixt[...].astype(BF16)
                pltpu.make_async_remote_copy(
                    src_ref=mix_out.at[f], dst_ref=mix_all.at[f, own_rows], send_sem=send_m, recv_sem=recv_m.at[f],
                    device_id=(i, sibling), device_id_type=MESH,
                ).start()

            @pl.when(n == 1)
            def _():
                mix_all[f, own_rows, :] = mixt[...].astype(BF16)
                pltpu.make_async_copy(mix_out.at[0], mix_out.at[0], recv_m.at[f]).wait()

                @pl.loop(0, 2)
                def _(b):
                    mixed = mix_all[f, :, pl.ds(pl.multiple_of(b * 256, 256), 256)].astype(F32).T.astype(BF16)
                    proj = dot(mixed, wo[...]).reshape(4, 2, 32, D)
                    devs = pl.ds(4 * b, 4)
                    for a in range(2):
                        at = pl.ds(pl.multiple_of(a * 64 + par * 32, 32), 32)
                        first = xin[f, devs, at, :].astype(F32) + gate * proj[:, a]
                        first_out[f, devs, a * 4 : a * 4 + 4] = first.reshape(4, 4, 8, D).astype(BF16)

                @pl.when(f == 0)
                def _():
                    pl.semaphore_wait(all_in, 7)

                slot = jnp.where(f == 0, i * 4 + y, 64 + i * 2 + y // 2)
                for dy, dz in YZ_FAR_FIRST:
                    for dc in range(2):
                        for k in range(2):
                            dx = (1 + core + 2 * k) % 4
                            to_x, to_z = (x + dx) % 4, (z + dz) % 4
                            dj = (y + dy) % 4 * 2 + (core + dc) % 2
                            src = first_out.at[f, dj, to_x // 2 * 4 + to_z]
                            copy = pltpu.make_async_remote_copy(
                                src_ref=src, dst_ref=recv_t.at[slot], send_sem=send_b,
                                recv_sem=recv_b.at[f], device_id=(to_x * 4 + to_z, dj), device_id_type=MESH,
                            )
                            if (dy, dz, dc, k) != (0, 0, 0, 1):
                                copy.start()
                            else:
                                pl.when(core == 0)(copy.start)

                @pl.when(core == 1)
                def _():
                    src = first_out.at[f, j, x // 2 * 4 + z]
                    pltpu.make_async_copy(src, recv_t.at[slot], recv_b.at[f]).start()

    weight_copy(wtq, wq, 3).wait()
    parts = ((0, 64, rows_a, qkv_a), (64, 32, rows_b, qkv_b))

    for f, (base, n, rows_f, qkv_f) in enumerate(parts):
        slots = recv_t.at[pl.ds(base, n)]
        pltpu.make_async_copy(slots, slots, recv_b.at[f]).wait()

        @pl.loop(0, n // 8)
        def _(c, base=base):
            rows = recv_t[pl.ds(base + c * 8, 8)].astype(F32).reshape(64, D)
            for b in range(9):
                f32_t[b, pl.ds(pl.multiple_of(base * 8 + c * 64, 64), 64), :] = rows[:, b * 128 : b * 128 + 128]

        @pl.loop(0, 8)
        def _(p, base=base, n=n, rows_f=rows_f):
            rows = jnp.concatenate([f32_t[b, pl.ds(base * 8 + p, n, stride=8), :] for b in range(9)], axis=1)
            at = pl.ds(pl.multiple_of(p * n, n), n)
            rows_f[at, :] = normed(rows, mods_t[0, base : base + n, :], mods_t[1, base : base + n, :])

        hidden = rows_f[...]
        qkv_f[:, :D] = (dot(hidden, wq[:, :D]) * Q_SCALE).astype(BF16)
        qkv_f[:, D : 2 * D] = dot(hidden, wq[:, D : 2 * D]).astype(BF16)
        qkv_f[:, 2 * D :] = dot(hidden, wq[:, 2 * D :]).astype(BF16)

    same = clip_col == clip_slots

    @pl.loop(0, 8)
    def _(p):
        at_a = pl.ds(pl.multiple_of(p * 64, 64), 64)
        at_b = pl.ds(pl.multiple_of(p * 32, 32), 32)
        blocks = [jnp.zeros((96, 128), F32) for _ in range(9)]
        for h in range(HEADS):
            off = window(h)
            lane = lax.broadcasted_iota(jnp.int32, (1, WIN), 1) + (off - h * HD)
            inside = jnp.logical_and(lane >= 0, lane < HD)

            def part(n):
                cols = slice(n * D + off, n * D + off + WIN)
                return jnp.concatenate([qkv_a[at_a, cols], qkv_b[at_b, cols]], axis=0)

            q = part(0)
            q = jnp.where(inside, q, jnp.zeros_like(q))
            scores = jnp.where(same, dot_t(q, part(1)), NEG)
            powers = jnp.exp2(scores - jnp.max(scores, axis=-1, keepdims=True))
            total = jnp.sum(powers, axis=-1, keepdims=True)
            out = dot(powers.astype(BF16), part(2)) * (1.0 / total)
            for b in range(off // 128, off // 128 + 2):
                lanes = slice(b * 128 - off, b * 128 - off + 128)
                blocks[b] = jnp.where(inside[:, lanes], out[:, lanes], blocks[b])
        for b in range(9):
            cols = slice(b * 128, b * 128 + 128)
            rows_a[at_a, cols] = blocks[b][:64].astype(BF16)
            rows_b[at_b, cols] = blocks[b][64:].astype(BF16)

    for f, (base, n, rows_f, _) in enumerate(parts):
        proj = dot(rows_f[...], wo2[...])
        for p in range(8):
            at = pl.ds(base * 8 + p, n, stride=8)
            for b in range(9):
                cols = slice(b * 128, b * 128 + 128)
                f32_t[b, at, :] = f32_t[b, at, :] + mods_t[2, base : base + n, cols] * proj[p * n : p * n + n, cols]

        @pl.loop(0, n // 8)
        def _(c, base=base):
            at = pl.ds(pl.multiple_of(base * 8 + c * 64, 64), 64)
            rows = jnp.concatenate([f32_t[b, at, :] for b in range(9)], axis=1)
            out_t[pl.ds(base + c * 8, 8)] = rows.reshape(8, 8, D).astype(BF16)

        size, start = (4, 0) if f == 0 else (2, 4)
        for dx, dz in XZ_FAR_FIRST:
            di = (x + dx) % 4 * 4 + (z + dz) % 4
            pltpu.make_async_remote_copy(
                src_ref=out_t.at[pl.ds(base + di * size, size)], dst_ref=final.at[pl.ds(start, size), i],
                send_sem=send_c, recv_sem=recv_c, device_id=(di, j), device_id_type=MESH,
            ).start()
        src = out_t.at[pl.ds(base + i * size, size)]
        pltpu.make_async_copy(src, final.at[pl.ds(start, size), i], recv_c).start()

    @pl.loop(0, 6 + 3 * count)
    def _(n):
        pltpu.make_async_copy(tokens.at[0], xin.at[0, 0], send_a).wait()

    @pl.loop(0, count)
    def _(n):
        pltpu.make_async_copy(mix_out.at[0], mix_out.at[0], send_m).wait()

    @pl.loop(0, count * (64 - core))
    def _(n):
        pltpu.make_async_copy(recv_t.at[0], recv_t.at[0], send_b).wait()

    @pl.loop(0, 15)
    def _(n):
        pltpu.make_async_copy(out_t.at[pl.ds(0, 6)], out_t.at[pl.ds(0, 6)], send_c).wait()

    pltpu.make_async_copy(final, final, recv_c).wait()


def body(tokens, clip_ids, modulation, w_spatial_qkv, w_spatial_out, w_temporal_qkv, w_temporal_out):
    any_, vmem = pl.BlockSpec(memory_space=pl.ANY), pl.BlockSpec(memory_space=pltpu.VMEM)
    dma = pltpu.SemaphoreType.DMA
    final = pl.pallas_call(
        kernel,
        out_shape=jax.ShapeDtypeStruct((6, 16, 8, D), BF16),
        in_specs=[any_, vmem, vmem, any_, any_, any_, any_],
        out_specs=any_,
        scratch_shapes=[
            pltpu.VMEM((2, 8, 128, D), BF16),
            pltpu.VMEM((D, 3 * D), BF16),
            pltpu.VMEM((D, D), BF16),
            pltpu.VMEM((D, D), BF16),
            pltpu.VMEM((WIDE, 128), F32),
            pltpu.VMEM((WIDE, 256), F32),
            pltpu.VMEM((HALF, WIN, 1024), BF16),
            pltpu.VMEM((1024, WIDE), BF16),
            pltpu.VMEM((HALF, HD + 8, 1024), BF16),
            pltpu.VMEM((2, 1024, 512), F32),
            pltpu.VMEM((2, 1024, 512), BF16),
            pltpu.VMEM((HALF * HD, 512), F32),
            pltpu.VMEM((2, HALF * HD, 512), BF16),
            pltpu.VMEM((2, D, 512), BF16),
            pltpu.VMEM((2, 8, 8, 8, D), BF16),
            pltpu.VMEM((96, 8, D), BF16),
            pltpu.VMEM((9, 768, 128), F32),
            pltpu.VMEM((512, D), BF16),
            pltpu.VMEM((256, D), BF16),
            pltpu.VMEM((512, 3 * D), BF16),
            pltpu.VMEM((256, 3 * D), BF16),
            pltpu.VMEM((96, 8, D), BF16),
            pltpu.VMEM((3, 96, D), F32),
            dma, dma((2, 8)), dma, dma((2,)), dma, dma((2,)), dma, dma, dma((4,)),
            pltpu.SemaphoreType.REGULAR,
        ],
        compiler_params=pltpu.CompilerParams(
            collective_id=0, has_side_effects=True, vmem_limit_bytes=63 * 1024 * 1024
        ),
        name="block",
    )(
        tokens, clip_ids.reshape(1, 96), modulation.transpose(1, 0, 2),
        w_spatial_qkv, w_spatial_out, w_temporal_qkv, w_temporal_out,
    )
    return final.reshape(6, 128, D)


def solution(mesh):
    in_specs = (P("frame", "inframe", None), P(), P(), P(), P(), P(), P())
    out_specs = P("frame", "inframe", None)
    return jax.shard_map(body, mesh=mesh, in_specs=in_specs, out_specs=out_specs, check_vma=False)
```

time: 133 us -> 128 us (0.962)
  the two profiles are of different devices: /device:TPU:14 before, /device:TPU:0 now
where the time goes in v3:
time: 128 us; the launch traced here: 127 us
  Pallas kernels  125 us (98%)
  local copies, waits for them, and re-layouts  2.82 us (2%)
    pallas_call x1, Pallas kernels, body(): pl.pallas_call(kernel, out_shape=jax.ShapeDtypeStruct((6, 16, 8, D), BF16...  125 us
    unnamed x1, local copies, waits for them, and re-layouts  2.82 us

profile of v3, /device:TPU:0, one launch (start us, length us, event | category | flops | bytes accessed | tf_op | source)
XLA Modules:
  0.0 127.4 jit_solution(13418493360739796142)
XLA Ops:
  0.0 124.6 %block.1 = bf16[6,16,8,1152]{3,2,1,0:T(8,128)(2,1)} custom-call(bf16[6,128,1152]{2,1,0:T(8,128)(2,1)} %tokens.1, s32[1,96]{1,0:T(1,128)} %bitcast.5, f32[6,4,1152]{2,1,0:T(4,128)} %bitcast.4, bf16[1152,3456]{1,0:T(8,128)(2,1)} %wsq.1, bf16[1152,1152]{1,0:T(8,128)(2,1)} %wso.1, bf16[1152,3456]{1,0:T(8,128)(2,1)} %wtq.1, bf16[1152,1152]{1,0:T(8,128)(2,1)} %wto.1), custom_call_target="tpu_custom_call" | custom-call | tf_op jit(solution)/shard_map/block/pallas_call | solution.py:371
  124.6 2.8 %copy.9 = bf16[6,128,1152]{2,1,0:T(8,128)(2,1)} copy(bf16[6,128,1152]{2,1,0:T(8,128)(2,1)} %bitcast.3) | data formatting | bytes 3538944

commit v4 on v3

v4 whole, which is shorter than its diff:
```python
import math

import jax
import jax.numpy as jnp
from jax import lax
from jax.experimental import pallas as pl
from jax.experimental.pallas import tpu as pltpu
from jax.sharding import PartitionSpec as P

MESH = pl.DeviceIdType.MESH
F32, BF16 = jnp.float32, jnp.bfloat16
HEADS = 16
HD = 72
D = HEADS * HD
WIN = 256
Q_SCALE = HD**-0.5 / math.log(2.0)
NEG = -1e30


def hops(*offsets):
    return sum(min(o, 4 - o) for o in offsets)


YZ_FAR_FIRST = sorted(((dy, dz) for dy in range(4) for dz in range(4)), key=lambda o: -hops(*o))
XZ_FAR_FIRST = YZ_FAR_FIRST[:-1]


def normed(x, shift, scale):
    center = x - jnp.mean(x, axis=-1, keepdims=True)
    spread = jnp.mean(center * center, axis=-1, keepdims=True)
    return (center * lax.rsqrt(spread + 1e-06) * (1.0 + scale) + shift).astype(BF16)


def dot(a, b):
    return jnp.dot(a, b, preferred_element_type=F32)


def dot_t(a, b):
    return lax.dot_general(a, b, (((1,), (1,)), ((), ())), preferred_element_type=F32)


def window(h):
    return min(h * HD // 128, 7) * 128


def kernel(
    tokens, clips, mod, wsq, wso, wtq, wto,
    final,
    xin, wq, wo, wo2, qtf, vtf, qt_s, k_s, vt_s, score, power, mixt, mix_out_0, mix_out_1, mix_0, mix_1,
    first_out, recv_t, f32_t,
    rows_a, rows_b, qkv_a, qkv_b, out_t, mods_t,
    send_a, recv_a, send_f, send_m, recv_m, send_b, recv_b, send_c, recv_c, w_sem, all_in,
):
    i = lax.axis_index("frame")
    j = lax.axis_index("inframe")
    x, z = i // 4, i % 4
    y, core = j // 2, j % 2
    sibling = y * 2 + 1 - core

    pair, member = y // 2, y % 2

    def weight_copy(src, dst, n):
        return pltpu.make_async_copy(src, dst, w_sem.at[n])

    barrier = pltpu.get_barrier_semaphore()

    @pl.loop(1, 8)
    def _(k):
        pl.semaphore_signal(barrier, inc=1, device_id=(i, (j + k) % 8), device_id_type=MESH)

    @pl.loop(1, 16)
    def _(k):
        pl.semaphore_signal(barrier, inc=1, device_id=((i + k) % 16, j), device_id_type=MESH)

    weight_copy(wsq, wq, 0).start()
    weight_copy(wso, wo, 1).start()
    weight_copy(wto, wo2, 2).start()
    pl.semaphore_wait(barrier, 22)

    def token_copy(src, f, block, dest):
        return pltpu.make_async_remote_copy(
            src_ref=src, dst_ref=xin.at[f, block], send_sem=send_a.at[f], recv_sem=recv_a.at[f, block],
            device_id=(i, dest), device_id_type=MESH,
        )

    def send_tokens(f):
        def owned(chip):
            return chip if f == 0 else 4 + chip // 2

        for dy in (2, 1, 3):
            chip = (y + dy) % 4
            token_copy(tokens.at[owned(chip)], f, j, chip * 2 + core).start()
        token_copy(tokens.at[owned(y)], f, j, sibling).start()
        pltpu.make_async_copy(tokens.at[owned(y)], xin.at[f, j], recv_a.at[f, j]).start()

    send_tokens(0)

    @pl.loop(1, 8)
    def _(k):
        pl.semaphore_signal(all_in, inc=1, device_id=(i, (j + k) % 8), device_id_type=MESH)

    def frame_at(slot):
        late = slot - 64
        return jnp.where(slot < 64, slot // 4 * 6 + slot % 4, late // 2 * 6 + 4 + late % 2)

    clip_row = clips[...]
    row_id = lax.broadcasted_iota(jnp.int32, (96, 96), 0)
    col_id = lax.broadcasted_iota(jnp.int32, (96, 96), 1)
    clip_rows = jnp.broadcast_to(clip_row, (96, 96))
    clip_natural = jnp.sum(jnp.where(row_id == col_id, clip_rows, 0), axis=1, keepdims=True)
    clip_col = jnp.sum(jnp.where(frame_at(row_id) == col_id, clip_rows, 0), axis=1, keepdims=True)
    clip_slots = jnp.sum(jnp.where(row_id == frame_at(col_id), clip_natural, 0), axis=0, keepdims=True)

    @pl.loop(0, 3)
    def _(n):
        picked = jnp.zeros((96, D), F32)
        for c in range(4):
            picked = jnp.where(clip_col == c, mod[3 + n, c : c + 1, :], picked)
        mods_t[n] = picked

    vt_s[:, HD:, :] = jnp.ones((HEADS // 2, 8, 1024), BF16)

    weight_copy(wsq, wq, 0).wait()
    weight_copy(wso, wo, 1).wait()
    weight_copy(wto, wo2, 2).wait()

    def spatial(f):
        heads, wide = (8, 640) if f == 0 else (4, 384)
        share = core if f == 0 else member * 2 + core
        features = heads * HD
        lane_gap = 512 if f == 0 else 256
        first_lane = pl.multiple_of(share * lane_gap, 256)
        frame = i * 6 + (y if f == 0 else 4 + pair)
        own_clip = jnp.sum(jnp.where(lane96 == frame, clip_row, 0), axis=1, keepdims=True)

        def own_mod(n):
            picked = jnp.zeros((1, D), F32)
            for c in range(4):
                picked = jnp.where(own_clip == c, mod[n, c : c + 1, :], picked)
            return picked

        shift, scale, gate = own_mod(0), own_mod(1), own_mod(2)

        def place(h):
            low = share * (features - lane_gap) + h * HD
            return low, pl.multiple_of(jnp.minimum(low // 128, wide // 128 - 2) * 128, 128)

        @pl.loop(0, 4)
        def _(s):
            yy = (y + jnp.where(s == 0, 0, jnp.where(s == 1, 2, jnp.where(s == 2, 1, 3)))) % 4

            if f == 0:
                @pl.when(s == 1)
                def _():
                    for _ in range(4):
                        pltpu.make_async_copy(tokens.at[0], xin.at[0, 0], send_a.at[0]).wait()
                    send_tokens(1)

            def arrived(block):
                pltpu.make_async_copy(tokens.at[0], xin.at[f, block], recv_a.at[f, block]).wait()

            arrived(yy * 2 + core)

            @pl.when(s > 0)
            def _():
                pltpu.make_async_remote_copy(
                    src_ref=xin.at[f, yy * 2 + core], dst_ref=xin.at[f, yy * 2 + core], send_sem=send_f,
                    recv_sem=recv_a.at[f, yy * 2 + core], device_id=(i, sibling), device_id_type=MESH,
                ).start()

            arrived(yy * 2 + 1 - core)
            rows = xin[f, pl.ds(2 * yy, 2)].astype(F32).reshape(256, D)
            hidden = normed(rows, shift, scale)
            at = pl.ds(pl.multiple_of(yy * 256, 256), 256)

            def project(n):
                return dot(hidden, wq[:, pl.ds(pl.multiple_of(n * D + first_lane, 128), wide)])

            q = (project(0) * Q_SCALE).reshape(2, 2, 2, 32, wide)
            for par in range(2):
                qtf[:wide] = q[:, :, par].reshape(128, wide).T
                cols = pl.ds(pl.multiple_of(par * 512 + yy * 128, 128), 128)
                for h in range(heads):
                    low, off = place(h)
                    row = lax.broadcasted_iota(jnp.int32, (WIN, 1), 0) + (off - low)
                    inside = jnp.logical_and(row >= 0, row < HD)
                    qt_s[h, :, cols] = jnp.where(inside, qtf[pl.ds(off, WIN), :], 0.0).astype(BF16)
            k_s[at, :wide] = project(1).astype(BF16)
            vtf[:wide] = project(2).T
            for h in range(heads):
                low, _ = place(h)
                vt_s[h, :HD, at] = vtf[pl.ds(pl.multiple_of(low, 8), HD), :].astype(BF16)

        if f == 1:
            weight_copy(wtq, wq, 3).start()

        own_rows = pl.ds(pl.multiple_of(share * features, features), features)
        mix_f = mix_0 if f == 0 else mix_1

        def hand_over(src, dest):
            pltpu.make_async_remote_copy(
                src_ref=src, dst_ref=mix_f.at[own_rows], send_sem=send_m.at[f], recv_sem=recv_m.at[f],
                device_id=(i, dest), device_id_type=MESH,
            ).start()

        @pl.loop(0, 2)
        def _(n):
            par = (x + n - core + 2) % 2
            cols = pl.ds(pl.multiple_of(par * 512, 512), 512)

            def scores(h, buf):
                _, off = place(h)
                score[buf] = dot(k_s[:, pl.ds(off, WIN)], qt_s[h, :, cols])

            def attend(h, buf):
                values = score[buf]
                top = jnp.max(values, axis=0, keepdims=True)
                power[buf] = jnp.exp2(values - top).astype(BF16)
                out = dot(vt_s[h], power[buf])
                mixt[pl.ds(pl.multiple_of(h * HD, 8), HD), :] = out[:HD] * (1.0 / out[HD : HD + 1])

            scores(0, 0)

            @pl.loop(0, heads // 2)
            def _(u):
                scores(2 * u + 1, 1)
                attend(2 * u, 0)
                scores(jnp.minimum(2 * u + 2, heads - 1), 0)
                attend(2 * u + 1, 1)

            if f == 0:
                @pl.when(n == 0)
                def _():
                    mix_out_0[...] = mixt[...].astype(BF16)
                    hand_over(mix_out_0, sibling)

                @pl.when(n == 1)
                def _():
                    mix_0[own_rows, :] = mixt[...].astype(BF16)
            else:
                there = y + 1 - 2 * member

                @pl.when(n == 0)
                def _():
                    for b in range(2):
                        mix_out_1[b] = mixt[:features, b * 256 : b * 256 + 256].astype(BF16)
                        hand_over(mix_out_1.at[b], (pair * 2 + b) * 2 + 1 - core)

                @pl.when(n == 1)
                def _():
                    for b in range(2):
                        part = mixt[:features, b * 256 : b * 256 + 256].astype(BF16)

                        @pl.when(member == b)
                        def _(part=part):
                            mix_1[own_rows, :] = part

                        @pl.when(member != b)
                        def _(part=part):
                            mix_out_1[2] = part
                            hand_over(mix_out_1.at[2], there * 2 + core)

        arriving = mix_out_0 if f == 0 else mix_out_1
        pltpu.make_async_copy(arriving, arriving, recv_m.at[f]).wait()
        par = (x + core + 1) % 2

        def finish(b, mixed):
            proj = dot(mixed.astype(F32).T.astype(BF16), wo[...]).reshape(4, 2, 32, D)
            devs = pl.ds(4 * b, 4)
            for a in range(2):
                at = pl.ds(pl.multiple_of(a * 64 + par * 32, 32), 32)
                first = xin[f, devs, at, :].astype(F32) + gate * proj[:, a]
                first_out[f, devs, a * 4 : a * 4 + 4] = first.reshape(4, 4, 8, D).astype(BF16)

        if f == 0:
            @pl.loop(0, 2)
            def _(b):
                finish(b, mix_0[:, pl.ds(pl.multiple_of(b * 256, 256), 256)])

            pl.semaphore_wait(all_in, 7)
            to_chips = [((y + dy) % 4, dy == 0) for dy in (2, 1, 3, 0)]
        else:
            finish(member, mix_1[...])
            to_chips = [(member * 2, None), (member * 2 + 1, None)]

        slot = i * 4 + y if f == 0 else 64 + i * 2 + pair
        for dz in (2, 1, 3, 0):
            for chip, same_chip in to_chips:
                for dc in range(2):
                    for k in range(2):
                        to_x, to_z = (x + 1 + core + 2 * k) % 4, (z + dz) % 4
                        dj = chip * 2 + (core + dc) % 2
                        src = first_out.at[f, dj, to_x // 2 * 4 + to_z]
                        copy = pltpu.make_async_remote_copy(
                            src_ref=src, dst_ref=recv_t.at[slot], send_sem=send_b.at[f],
                            recv_sem=recv_b.at[f], device_id=(to_x * 4 + to_z, dj), device_id_type=MESH,
                        )
                        if dz or dc or k == 0 or same_chip is False:
                            copy.start()
                        else:
                            here = jnp.logical_and(core == 1, chip == y)
                            pl.when(jnp.logical_not(here))(copy.start)
                            pl.when(here)(pltpu.make_async_copy(src, recv_t.at[slot], recv_b.at[f]).start)

    lane96 = lax.broadcasted_iota(jnp.int32, (1, 96), 1)
    spatial(0)
    spatial(1)

    weight_copy(wtq, wq, 3).wait()
    parts = ((0, 64, rows_a, qkv_a), (64, 32, rows_b, qkv_b))

    for f, (base, n, rows_f, qkv_f) in enumerate(parts):
        slots = recv_t.at[pl.ds(base, n)]
        pltpu.make_async_copy(slots, slots, recv_b.at[f]).wait()

        @pl.loop(0, n // 8)
        def _(c, base=base):
            rows = recv_t[pl.ds(base + c * 8, 8)].astype(F32).reshape(64, D)
            for b in range(9):
                f32_t[b, pl.ds(pl.multiple_of(base * 8 + c * 64, 64), 64), :] = rows[:, b * 128 : b * 128 + 128]

        @pl.loop(0, 8)
        def _(p, base=base, n=n, rows_f=rows_f):
            rows = jnp.concatenate([f32_t[b, pl.ds(base * 8 + p, n, stride=8), :] for b in range(9)], axis=1)
            at = pl.ds(pl.multiple_of(p * n, n), n)
            rows_f[at, :] = normed(rows, mods_t[0, base : base + n, :], mods_t[1, base : base + n, :])

        hidden = rows_f[...]
        qkv_f[:, :D] = (dot(hidden, wq[:, :D]) * Q_SCALE).astype(BF16)
        qkv_f[:, D : 2 * D] = dot(hidden, wq[:, D : 2 * D]).astype(BF16)
        qkv_f[:, 2 * D :] = dot(hidden, wq[:, 2 * D :]).astype(BF16)

    same = clip_col == clip_slots

    for f, (base, n, rows_f, qkv_f) in enumerate(parts):
        @pl.loop(0, 8)
        def _(p, base=base, n=n, rows_f=rows_f, qkv_f=qkv_f):
            at = pl.ds(pl.multiple_of(p * n, n), n)
            at_a = pl.ds(pl.multiple_of(p * 64, 64), 64)
            at_b = pl.ds(pl.multiple_of(p * 32, 32), 32)
            blocks = [jnp.zeros((n, 128), F32) for _ in range(9)]
            for h in range(HEADS):
                off = window(h)
                lane = lax.broadcasted_iota(jnp.int32, (1, WIN), 1) + (off - h * HD)
                inside = jnp.logical_and(lane >= 0, lane < HD)

                def part(m):
                    cols = slice(m * D + off, m * D + off + WIN)
                    return jnp.concatenate([qkv_a[at_a, cols], qkv_b[at_b, cols]], axis=0)

                q = qkv_f[at, off : off + WIN]
                q = jnp.where(inside, q, jnp.zeros_like(q))
                scores = jnp.where(same[base : base + n], dot_t(q, part(1)), NEG)
                powers = jnp.exp2(scores - jnp.max(scores, axis=-1, keepdims=True))
                total = jnp.sum(powers, axis=-1, keepdims=True)
                out = dot(powers.astype(BF16), part(2)) * (1.0 / total)
                for b in range(off // 128, off // 128 + 2):
                    lanes = slice(b * 128 - off, b * 128 - off + 128)
                    blocks[b] = jnp.where(inside[:, lanes], out[:, lanes], blocks[b])
            for b in range(9):
                rows_f[at, b * 128 : b * 128 + 128] = blocks[b].astype(BF16)

        proj = dot(rows_f[...], wo2[...])
        for p in range(8):
            at = pl.ds(base * 8 + p, n, stride=8)
            for b in range(9):
                cols = slice(b * 128, b * 128 + 128)
                f32_t[b, at, :] = f32_t[b, at, :] + mods_t[2, base : base + n, cols] * proj[p * n : p * n + n, cols]

        @pl.loop(0, n // 8)
        def _(c, base=base):
            at = pl.ds(pl.multiple_of(base * 8 + c * 64, 64), 64)
            rows = jnp.concatenate([f32_t[b, at, :] for b in range(9)], axis=1)
            out_t[pl.ds(base + c * 8, 8)] = rows.reshape(8, 8, D).astype(BF16)

        size, start = (4, 0) if f == 0 else (2, 4)
        for dx, dz in XZ_FAR_FIRST:
            di = (x + dx) % 4 * 4 + (z + dz) % 4
            pltpu.make_async_remote_copy(
                src_ref=out_t.at[pl.ds(base + di * size, size)], dst_ref=final.at[pl.ds(start, size), i],
                send_sem=send_c, recv_sem=recv_c, device_id=(di, j), device_id_type=MESH,
            ).start()
        src = out_t.at[pl.ds(base + i * size, size)]
        pltpu.make_async_copy(src, final.at[pl.ds(start, size), i], recv_c).start()

    for _ in range(4):
        pltpu.make_async_copy(tokens.at[0], xin.at[0, 0], send_a.at[1]).wait()
    for _ in range(6):
        pltpu.make_async_copy(tokens.at[0], xin.at[0, 0], send_f).wait()
    pltpu.make_async_copy(mix_out_0, mix_out_0, send_m.at[0]).wait()
    for _ in range(3):
        pltpu.make_async_copy(mix_out_1.at[0], mix_out_1.at[0], send_m.at[1]).wait()

    @pl.loop(0, 64 - core)
    def _(n):
        pltpu.make_async_copy(recv_t.at[0], recv_t.at[0], send_b.at[0]).wait()

    self_sent = jnp.where(jnp.logical_and(core == 1, pair == member), 1, 0)

    @pl.loop(0, 32 - self_sent)
    def _(n):
        pltpu.make_async_copy(recv_t.at[0], recv_t.at[0], send_b.at[1]).wait()

    @pl.loop(0, 15)
    def _(n):
        pltpu.make_async_copy(out_t.at[pl.ds(0, 6)], out_t.at[pl.ds(0, 6)], send_c).wait()

    pltpu.make_async_copy(final, final, recv_c).wait()


def body(tokens, clip_ids, modulation, w_spatial_qkv, w_spatial_out, w_temporal_qkv, w_temporal_out):
    any_, vmem = pl.BlockSpec(memory_space=pl.ANY), pl.BlockSpec(memory_space=pltpu.VMEM)
    dma = pltpu.SemaphoreType.DMA
    final = pl.pallas_call(
        kernel,
        out_shape=jax.ShapeDtypeStruct((6, 16, 8, D), BF16),
        in_specs=[any_, vmem, vmem, any_, any_, any_, any_],
        out_specs=any_,
        scratch_shapes=[
            pltpu.VMEM((2, 8, 128, D), BF16),
            pltpu.VMEM((D, 3 * D), BF16),
            pltpu.VMEM((D, D), BF16),
            pltpu.VMEM((D, D), BF16),
            pltpu.VMEM((640, 128), F32),
            pltpu.VMEM((640, 256), F32),
            pltpu.VMEM((HEADS // 2, WIN, 1024), BF16),
            pltpu.VMEM((1024, 640), BF16),
            pltpu.VMEM((HEADS // 2, HD + 8, 1024), BF16),
            pltpu.VMEM((2, 1024, 512), F32),
            pltpu.VMEM((2, 1024, 512), BF16),
            pltpu.VMEM((D // 2, 512), F32),
            pltpu.VMEM((D // 2, 512), BF16),
            pltpu.VMEM((3, D // 4, 256), BF16),
            pltpu.VMEM((D, 512), BF16),
            pltpu.VMEM((D, 256), BF16),
            pltpu.VMEM((2, 8, 8, 8, D), BF16),
            pltpu.VMEM((96, 8, D), BF16),
            pltpu.VMEM((9, 768, 128), F32),
            pltpu.VMEM((512, D), BF16),
            pltpu.VMEM((256, D), BF16),
            pltpu.VMEM((512, 3 * D), BF16),
            pltpu.VMEM((256, 3 * D), BF16),
            pltpu.VMEM((96, 8, D), BF16),
            pltpu.VMEM((3, 96, D), F32),
            dma((2,)), dma((2, 8)), dma, dma((2,)), dma((2,)), dma((2,)), dma((2,)), dma, dma, dma((4,)),
            pltpu.SemaphoreType.REGULAR,
        ],
        compiler_params=pltpu.CompilerParams(
            collective_id=0, has_side_effects=True, vmem_limit_bytes=63 * 1024 * 1024
        ),
        name="block",
    )(
        tokens, clip_ids.reshape(1, 96), modulation.transpose(1, 0, 2),
        w_spatial_qkv, w_spatial_out, w_temporal_qkv, w_temporal_out,
    )
    return final.reshape(6, 128, D)


def solution(mesh):
    in_specs = (P("frame", "inframe", None), P(), P(), P(), P(), P(), P())
    out_specs = P("frame", "inframe", None)
    return jax.shard_map(body, mesh=mesh, in_specs=in_specs, out_specs=out_specs, check_vma=False)
```

time: 128 us -> 163 us (1.27)
  Pallas kernels: 125 us -> 160 us
    pallas_call x1, Pallas kernels: 125 us -> 160 us  [body(): pl.pallas_call(kernel, out_shape=jax.ShapeDtypeStruct((6, 16, 8, D), BF16...]
where the time goes in v4:
time: 163 us
  Pallas kernels  160 us (98%)
  local copies, waits for them, and re-layouts  2.82 us (2%)
    pallas_call x1, Pallas kernels, body(): pl.pallas_call(kernel, out_shape=jax.ShapeDtypeStruct((6, 16, 8, D), BF16...  160 us

profile of v4, /device:TPU:0, one launch (start us, length us, event | category | flops | bytes accessed | tf_op | source)
XLA Modules:
  0.0 163.1 jit_solution(17915067339798856236)
XLA Ops:
  0.0 160.3 %block.1 = bf16[6,16,8,1152]{3,2,1,0:T(8,128)(2,1)} custom-call(bf16[6,128,1152]{2,1,0:T(8,128)(2,1)} %tokens.1, s32[1,96]{1,0:T(1,128)} %bitcast.5, f32[6,4,1152]{2,1,0:T(4,128)} %bitcast.4, bf16[1152,3456]{1,0:T(8,128)(2,1)} %wsq.1, bf16[1152,1152]{1,0:T(8,128)(2,1)} %wso.1, bf16[1152,3456]{1,0:T(8,128)(2,1)} %wtq.1, bf16[1152,1152]{1,0:T(8,128)(2,1)} %wto.1), custom_call_target="tpu_custom_call" | custom-call | tf_op jit(solution)/shard_map/block/pallas_call | solution.py:414
  160.3 2.8 %copy.9 = bf16[6,128,1152]{2,1,0:T(8,128)(2,1)} copy(bf16[6,128,1152]{2,1,0:T(8,128)(2,1)} %bitcast.3) | data formatting | bytes 3538944

commit v5 on v4

--- a/solution.py
+++ b/solution.py
@@ -17,11 +17,8 @@
 NEG = -1e30
 
 
-def hops(*offsets):
-    return sum(min(o, 4 - o) for o in offsets)
-
-
-YZ_FAR_FIRST = sorted(((dy, dz) for dy in range(4) for dz in range(4)), key=lambda o: -hops(*o))
+YZ_FAR_FIRST = [(2, 2), (1, 2), (2, 1), (3, 2), (2, 3), (1, 1), (3, 3), (1, 3), (3, 1), (2, 0), (0, 2)]
+YZ_FAR_FIRST += [(1, 0), (0, 1), (3, 0), (0, 3), (0, 0)]
 XZ_FAR_FIRST = YZ_FAR_FIRST[:-1]
 
 
@@ -46,9 +43,9 @@
 def kernel(
     tokens, clips, mod, wsq, wso, wtq, wto,
     final,
-    xin, wq, wo, wo2, qtf, vtf, qt_s, k_s, vt_s, score, power, mixt, mix_out_0, mix_out_1, mix_0, mix_1,
+    xin, wq, ws, wo, wo2, qtf, vtf, qt_s, k_s, vt_s, score, power, mixt, mix_out_0, mix_out_1, mix_0, mix_1,
     first_out, recv_t, f32_t,
-    rows_a, rows_b, qkv_a, qkv_b, out_t, mods_t,
+    rows_a, rows_b, qkv_a, qkv_b, mods_t,
     send_a, recv_a, send_f, send_m, recv_m, send_b, recv_b, send_c, recv_c, w_sem, all_in,
 ):
     i = lax.axis_index("frame")
@@ -72,9 +69,22 @@
     def _(k):
         pl.semaphore_signal(barrier, inc=1, device_id=((i + k) % 16, j), device_id_type=MESH)
 
-    weight_copy(wsq, wq, 0).start()
-    weight_copy(wso, wo, 1).start()
-    weight_copy(wto, wo2, 2).start()
+    def head_columns(f):
+        wide, lane_gap = (640, 512) if f == 0 else (384, 256)
+        share = core if f == 0 else member * 2 + core
+        return [
+            weight_copy(
+                wsq.at[:, pl.ds(pl.multiple_of(n * D + share * lane_gap, 128), wide)],
+                ws.at[:, n * wide : n * wide + wide], 3 * f + n,
+            )
+            for n in range(3)
+        ]
+
+    for copy in head_columns(0):
+        copy.start()
+    weight_copy(wso, wo, 6).start()
+    weight_copy(wto, wo2, 7).start()
+    weight_copy(wtq, wq, 8).start()
     pl.semaphore_wait(barrier, 22)
 
     def token_copy(src, f, block, dest):
@@ -120,16 +130,29 @@
 
     vt_s[:, HD:, :] = jnp.ones((HEADS // 2, 8, 1024), BF16)
 
-    weight_copy(wsq, wq, 0).wait()
-    weight_copy(wso, wo, 1).wait()
-    weight_copy(wto, wo2, 2).wait()
+    for copy in head_columns(0):
+        copy.wait()
+    weight_copy(wso, wo, 6).wait()
+    weight_copy(wto, wo2, 7).wait()
+    weight_copy(wtq, wq, 8).wait()
+
+    def arrived(f, block):
+        pltpu.make_async_copy(tokens.at[0], xin.at[f, block], recv_a.at[f, block]).wait()
+
+    def forward(f):
+        for dy in (2, 1, 3):
+            block = (y + dy) % 4 * 2 + core
+            arrived(f, block)
+            pltpu.make_async_remote_copy(
+                src_ref=xin.at[f, block], dst_ref=xin.at[f, block], send_sem=send_f,
+                recv_sem=recv_a.at[f, block], device_id=(i, sibling), device_id_type=MESH,
+            ).start()
 
     def spatial(f):
         heads, wide = (8, 640) if f == 0 else (4, 384)
         share = core if f == 0 else member * 2 + core
         features = heads * HD
         lane_gap = 512 if f == 0 else 256
-        first_lane = pl.multiple_of(share * lane_gap, 256)
         frame = i * 6 + (y if f == 0 else 4 + pair)
         own_clip = jnp.sum(jnp.where(lane96 == frame, clip_row, 0), axis=1, keepdims=True)
 
@@ -144,6 +167,11 @@
         def place(h):
             low = share * (features - lane_gap) + h * HD
             return low, pl.multiple_of(jnp.minimum(low // 128, wide // 128 - 2) * 128, 128)
+
+        arrived(f, j)
+        if f == 1:
+            for copy in head_columns(1):
+                copy.wait()
 
         @pl.loop(0, 4)
         def _(s):
@@ -155,28 +183,15 @@
                     for _ in range(4):
                         pltpu.make_async_copy(tokens.at[0], xin.at[0, 0], send_a.at[0]).wait()
                     send_tokens(1)
-
-            def arrived(block):
-                pltpu.make_async_copy(tokens.at[0], xin.at[f, block], recv_a.at[f, block]).wait()
-
-            arrived(yy * 2 + core)
-
-            @pl.when(s > 0)
-            def _():
-                pltpu.make_async_remote_copy(
-                    src_ref=xin.at[f, yy * 2 + core], dst_ref=xin.at[f, yy * 2 + core], send_sem=send_f,
-                    recv_sem=recv_a.at[f, yy * 2 + core], device_id=(i, sibling), device_id_type=MESH,
-                ).start()
-
-            arrived(yy * 2 + 1 - core)
+                    forward(0)
+
+            arrived(f, yy * 2 + 1 - core)
             rows = xin[f, pl.ds(2 * yy, 2)].astype(F32).reshape(256, D)
             hidden = normed(rows, shift, scale)
             at = pl.ds(pl.multiple_of(yy * 256, 256), 256)
 
-            def project(n):
-                return dot(hidden, wq[:, pl.ds(pl.multiple_of(n * D + first_lane, 128), wide)])
-
-            q = (project(0) * Q_SCALE).reshape(2, 2, 2, 32, wide)
+            qkv = dot(hidden, ws[:, : 3 * wide])
+            q = (qkv[:, :wide] * Q_SCALE).reshape(2, 2, 2, 32, wide)
             for par in range(2):
                 qtf[:wide] = q[:, :, par].reshape(128, wide).T
                 cols = pl.ds(pl.multiple_of(par * 512 + yy * 128, 128), 128)
@@ -185,14 +200,15 @@
                     row = lax.broadcasted_iota(jnp.int32, (WIN, 1), 0) + (off - low)
                     inside = jnp.logical_and(row >= 0, row < HD)
                     qt_s[h, :, cols] = jnp.where(inside, qtf[pl.ds(off, WIN), :], 0.0).astype(BF16)
-            k_s[at, :wide] = project(1).astype(BF16)
-            vtf[:wide] = project(2).T
+            k_s[at, :wide] = qkv[:, wide : 2 * wide].astype(BF16)
+            vtf[:wide] = qkv[:, 2 * wide :].T
             for h in range(heads):
                 low, _ = place(h)
                 vt_s[h, :HD, at] = vtf[pl.ds(pl.multiple_of(low, 8), HD), :].astype(BF16)
 
-        if f == 1:
-            weight_copy(wtq, wq, 3).start()
+        if f == 0:
+            for copy in head_columns(1):
+                copy.start()
 
         own_rows = pl.ds(pl.multiple_of(share * features, features), features)
         mix_f = mix_0 if f == 0 else mix_1
@@ -260,6 +276,8 @@
                             mix_out_1[2] = part
                             hand_over(mix_out_1.at[2], there * 2 + core)
 
+        if f == 0:
+            forward(1)
         arriving = mix_out_0 if f == 0 else mix_out_1
         pltpu.make_async_copy(arriving, arriving, recv_m.at[f]).wait()
         par = (x + core + 1) % 2
@@ -278,35 +296,33 @@
                 finish(b, mix_0[:, pl.ds(pl.multiple_of(b * 256, 256), 256)])
 
             pl.semaphore_wait(all_in, 7)
-            to_chips = [((y + dy) % 4, dy == 0) for dy in (2, 1, 3, 0)]
+            targets = [((y + dy) % 4, dz, dy == 0) for dy, dz in YZ_FAR_FIRST]
         else:
             finish(member, mix_1[...])
-            to_chips = [(member * 2, None), (member * 2 + 1, None)]
+            targets = [(member * 2 + e, dz, True) for dz in (2, 1, 3, 0) for e in range(2)]
 
         slot = i * 4 + y if f == 0 else 64 + i * 2 + pair
-        for dz in (2, 1, 3, 0):
-            for chip, same_chip in to_chips:
+        for chip, dz, may_be_here in targets:
+            for k in range(2):
                 for dc in range(2):
-                    for k in range(2):
-                        to_x, to_z = (x + 1 + core + 2 * k) % 4, (z + dz) % 4
-                        dj = chip * 2 + (core + dc) % 2
-                        src = first_out.at[f, dj, to_x // 2 * 4 + to_z]
-                        copy = pltpu.make_async_remote_copy(
-                            src_ref=src, dst_ref=recv_t.at[slot], send_sem=send_b.at[f],
-                            recv_sem=recv_b.at[f], device_id=(to_x * 4 + to_z, dj), device_id_type=MESH,
-                        )
-                        if dz or dc or k == 0 or same_chip is False:
-                            copy.start()
-                        else:
-                            here = jnp.logical_and(core == 1, chip == y)
-                            pl.when(jnp.logical_not(here))(copy.start)
-                            pl.when(here)(pltpu.make_async_copy(src, recv_t.at[slot], recv_b.at[f]).start)
+                    to_x, to_z = (x + 1 + core + 2 * k) % 4, (z + dz) % 4
+                    dj = chip * 2 + (core + dc) % 2
+                    src = first_out.at[f, dj, to_x // 2 * 4 + to_z]
+                    copy = pltpu.make_async_remote_copy(
+                        src_ref=src, dst_ref=recv_t.at[slot], send_sem=send_b.at[f],
+                        recv_sem=recv_b.at[f], device_id=(to_x * 4 + to_z, dj), device_id_type=MESH,
+                    )
+                    if dz or dc or k == 0 or not may_be_here:
+                        copy.start()
+                    else:
+                        here = jnp.logical_and(core == 1, chip == y)
+                        pl.when(jnp.logical_not(here))(copy.start)
+                        pl.when(here)(pltpu.make_async_copy(src, recv_t.at[slot], recv_b.at[f]).start)
 
     lane96 = lax.broadcasted_iota(jnp.int32, (1, 96), 1)
     spatial(0)
     spatial(1)
 
-    weight_copy(wtq, wq, 3).wait()
     parts = ((0, 64, rows_a, qkv_a), (64, 32, rows_b, qkv_b))
 
     for f, (base, n, rows_f, qkv_f) in enumerate(parts):
@@ -327,39 +343,43 @@
 
         hidden = rows_f[...]
         qkv_f[:, :D] = (dot(hidden, wq[:, :D]) * Q_SCALE).astype(BF16)
-        qkv_f[:, D : 2 * D] = dot(hidden, wq[:, D : 2 * D]).astype(BF16)
-        qkv_f[:, 2 * D :] = dot(hidden, wq[:, 2 * D :]).astype(BF16)
+        qkv_f[:, D:] = dot(hidden, wq[:, D:]).astype(BF16)
 
     same = clip_col == clip_slots
 
-    for f, (base, n, rows_f, qkv_f) in enumerate(parts):
-        @pl.loop(0, 8)
-        def _(p, base=base, n=n, rows_f=rows_f, qkv_f=qkv_f):
-            at = pl.ds(pl.multiple_of(p * n, n), n)
-            at_a = pl.ds(pl.multiple_of(p * 64, 64), 64)
-            at_b = pl.ds(pl.multiple_of(p * 32, 32), 32)
-            blocks = [jnp.zeros((n, 128), F32) for _ in range(9)]
-            for h in range(HEADS):
-                off = window(h)
-                lane = lax.broadcasted_iota(jnp.int32, (1, WIN), 1) + (off - h * HD)
-                inside = jnp.logical_and(lane >= 0, lane < HD)
-
-                def part(m):
-                    cols = slice(m * D + off, m * D + off + WIN)
-                    return jnp.concatenate([qkv_a[at_a, cols], qkv_b[at_b, cols]], axis=0)
-
-                q = qkv_f[at, off : off + WIN]
-                q = jnp.where(inside, q, jnp.zeros_like(q))
-                scores = jnp.where(same[base : base + n], dot_t(q, part(1)), NEG)
-                powers = jnp.exp2(scores - jnp.max(scores, axis=-1, keepdims=True))
-                total = jnp.sum(powers, axis=-1, keepdims=True)
-                out = dot(powers.astype(BF16), part(2)) * (1.0 / total)
-                for b in range(off // 128, off // 128 + 2):
-                    lanes = slice(b * 128 - off, b * 128 - off + 128)
-                    blocks[b] = jnp.where(inside[:, lanes], out[:, lanes], blocks[b])
-            for b in range(9):
-                rows_f[at, b * 128 : b * 128 + 128] = blocks[b].astype(BF16)
-
+    def attend_position(p):
+        at_a = pl.ds(pl.multiple_of(p * 64, 64), 64)
+        at_b = pl.ds(pl.multiple_of(p * 32, 32), 32)
+        blocks = [jnp.zeros((96, 128), F32) for _ in range(9)]
+        for h in range(HEADS):
+            off = window(h)
+            lane = lax.broadcasted_iota(jnp.int32, (1, WIN), 1) + (off - h * HD)
+            inside = jnp.logical_and(lane >= 0, lane < HD)
+
+            def part(m):
+                cols = slice(m * D + off, m * D + off + WIN)
+                return jnp.concatenate([qkv_a[at_a, cols], qkv_b[at_b, cols]], axis=0)
+
+            q = part(0)
+            q = jnp.where(inside, q, jnp.zeros_like(q))
+            scores = jnp.where(same, dot_t(q, part(1)), NEG)
+            powers = jnp.exp2(scores - jnp.max(scores, axis=-1, keepdims=True))
+            total = jnp.sum(powers, axis=-1, keepdims=True)
+            out = dot(powers.astype(BF16), part(2)) * (1.0 / total)
+            for b in range(off // 128, off // 128 + 2):
+                lanes = slice(b * 128 - off, b * 128 - off + 128)
+                blocks[b] = jnp.where(inside[:, lanes], out[:, lanes], blocks[b])
+        for b in range(9):
+            cols = slice(b * 128, b * 128 + 128)
+            rows_a[at_a, cols] = blocks[b][:64].astype(BF16)
+            rows_b[at_b, cols] = blocks[b][64:].astype(BF16)
+
+    @pl.loop(0, 4)
+    def _(u):
+        attend_position(2 * u)
+        attend_position(2 * u + 1)
+
+    for f, (base, n, rows_f, _) in enumerate(parts):
         proj = dot(rows_f[...], wo2[...])
         for p in range(8):
             at = pl.ds(base * 8 + p, n, stride=8)
@@ -371,16 +391,16 @@
         def _(c, base=base):
             at = pl.ds(pl.multiple_of(base * 8 + c * 64, 64), 64)
             rows = jnp.concatenate([f32_t[b, at, :] for b in range(9)], axis=1)
-            out_t[pl.ds(base + c * 8, 8)] = rows.reshape(8, 8, D).astype(BF16)
+            recv_t[pl.ds(base + c * 8, 8)] = rows.reshape(8, 8, D).astype(BF16)
 
         size, start = (4, 0) if f == 0 else (2, 4)
         for dx, dz in XZ_FAR_FIRST:
             di = (x + dx) % 4 * 4 + (z + dz) % 4
             pltpu.make_async_remote_copy(
-                src_ref=out_t.at[pl.ds(base + di * size, size)], dst_ref=final.at[pl.ds(start, size), i],
+                src_ref=recv_t.at[pl.ds(base + di * size, size)], dst_ref=final.at[pl.ds(start, size), i],
                 send_sem=send_c, recv_sem=recv_c, device_id=(di, j), device_id_type=MESH,
             ).start()
-        src = out_t.at[pl.ds(base + i * size, size)]
+        src = recv_t.at[pl.ds(base + i * size, size)]
         pltpu.make_async_copy(src, final.at[pl.ds(start, size), i], recv_c).start()
 
     for _ in range(4):
@@ -403,7 +423,7 @@
 
     @pl.loop(0, 15)
     def _(n):
-        pltpu.make_async_copy(out_t.at[pl.ds(0, 6)], out_t.at[pl.ds(0, 6)], send_c).wait()
+        pltpu.make_async_copy(recv_t.at[pl.ds(0, 6)], recv_t.at[pl.ds(0, 6)], send_c).wait()
 
     pltpu.make_async_copy(final, final, recv_c).wait()
 
@@ -419,6 +439,7 @@
         scratch_shapes=[
             pltpu.VMEM((2, 8, 128, D), BF16),
             pltpu.VMEM((D, 3 * D), BF16),
+            pltpu.VMEM((D, 1920), BF16),
             pltpu.VMEM((D, D), BF16),
             pltpu.VMEM((D, D), BF16),
             pltpu.VMEM((640, 128), F32),
@@ -440,9 +461,8 @@
             pltpu.VMEM((256, D), BF16),
             pltpu.VMEM((512, 3 * D), BF16),
             pltpu.VMEM((256, 3 * D), BF16),
-            pltpu.VMEM((96, 8, D), BF16),
             pltpu.VMEM((3, 96, D), F32),
-            dma((2,)), dma((2, 8)), dma, dma((2,)), dma((2,)), dma((2,)), dma((2,)), dma, dma, dma((4,)),
+            dma((2,)), dma((2, 8)), dma, dma((2,)), dma((2,)), dma((2,)), dma((2,)), dma, dma, dma((9,)),
             pltpu.SemaphoreType.REGULAR,
         ],
         compiler_params=pltpu.CompilerParams(

time: 163 us -> 117 us (0.72)
  Pallas kernels: 160 us -> 113 us
    pallas_call x1, Pallas kernels: 160 us -> 113 us  [body(): pl.pallas_call(kernel, out_shape=jax.ShapeDtypeStruct((6, 16, 8, D), BF16...]
where the time goes in v5:
time: 117 us; the launch traced here: 116 us
  Pallas kernels  113 us (97%)
  local copies, waits for them, and re-layouts  2.82 us (2%)
    pallas_call x1, Pallas kernels, body(): pl.pallas_call(kernel, out_shape=jax.ShapeDtypeStruct((6, 16, 8, D), BF16...  113 us
    unnamed x1, local copies, waits for them, and re-layouts  2.82 us

profile of v5, /device:TPU:0, one launch (start us, length us, event | category | flops | bytes accessed | tf_op | source)
XLA Modules:
  0.0 116.1 jit_solution(16820786306540372579)
XLA Ops:
  0.0 113.3 %block.1 = bf16[6,16,8,1152]{3,2,1,0:T(8,128)(2,1)} custom-call(bf16[6,128,1152]{2,1,0:T(8,128)(2,1)} %tokens.1, s32[1,96]{1,0:T(1,128)} %bitcast.5, f32[6,4,1152]{2,1,0:T(4,128)} %bitcast.4, bf16[1152,3456]{1,0:T(8,128)(2,1)} %wsq.1, bf16[1152,1152]{1,0:T(8,128)(2,1)} %wso.1, bf16[1152,3456]{1,0:T(8,128)(2,1)} %wtq.1, bf16[1152,1152]{1,0:T(8,128)(2,1)} %wto.1), custom_call_target="tpu_custom_call" | custom-call | tf_op jit(solution)/shard_map/block/pallas_call | solution.py:434
  113.3 2.8 %copy.9 = bf16[6,128,1152]{2,1,0:T(8,128)(2,1)} copy(bf16[6,128,1152]{2,1,0:T(8,128)(2,1)} %bitcast.3) | data formatting | bytes 3538944

commit v6 on v5

--- a/solution.py
+++ b/solution.py
@@ -148,6 +148,26 @@
                 recv_sem=recv_a.at[f, block], device_id=(i, sibling), device_id_type=MESH,
             ).start()
 
+    def send_first(f, targets):
+        slot = i * 4 + y if f == 0 else 64 + i * 2 + pair
+        for place_y, dz in targets:
+            chip = (y + place_y) % 4 if f == 0 else member * 2 + place_y
+            for k in range(2):
+                for dc in range(2):
+                    to_x, to_z = (x + 1 + core + 2 * k) % 4, (z + dz) % 4
+                    dj = chip * 2 + (core + dc) % 2
+                    src = first_out.at[f, dj, to_x // 2 * 4 + to_z]
+                    copy = pltpu.make_async_remote_copy(
+                        src_ref=src, dst_ref=recv_t.at[slot], send_sem=send_b.at[f],
+                        recv_sem=recv_b.at[f], device_id=(to_x * 4 + to_z, dj), device_id_type=MESH,
+                    )
+                    if dz or dc or k == 0 or (f == 0 and place_y):
+                        copy.start()
+                    else:
+                        here = jnp.logical_and(core == 1, chip == y)
+                        pl.when(jnp.logical_not(here))(copy.start)
+                        pl.when(here)(pltpu.make_async_copy(src, recv_t.at[slot], recv_b.at[f]).start)
+
     def spatial(f):
         heads, wide = (8, 640) if f == 0 else (4, 384)
         share = core if f == 0 else member * 2 + core
@@ -194,7 +214,8 @@
             q = (qkv[:, :wide] * Q_SCALE).reshape(2, 2, 2, 32, wide)
             for par in range(2):
                 qtf[:wide] = q[:, :, par].reshape(128, wide).T
-                cols = pl.ds(pl.multiple_of(par * 512 + yy * 128, 128), 128)
+                start = par * 512 + yy * 128 if f == 0 else yy // 2 * 512 + par * 256 + yy % 2 * 128
+                cols = pl.ds(pl.multiple_of(start, 128), 128)
                 for h in range(heads):
                     low, off = place(h)
                     row = lax.broadcasted_iota(jnp.int32, (WIN, 1), 0) + (off - low)
@@ -221,8 +242,8 @@
 
         @pl.loop(0, 2)
         def _(n):
-            par = (x + n - core + 2) % 2
-            cols = pl.ds(pl.multiple_of(par * 512, 512), 512)
+            block = (x + n - core + 2) % 2 if f == 0 else (member + 1 + n) % 2
+            cols = pl.ds(pl.multiple_of(block * 512, 512), 512)
 
             def scores(h, buf):
                 _, off = place(h)
@@ -255,26 +276,23 @@
                     mix_0[own_rows, :] = mixt[...].astype(BF16)
             else:
                 there = y + 1 - 2 * member
-
-                @pl.when(n == 0)
-                def _():
-                    for b in range(2):
-                        mix_out_1[b] = mixt[:features, b * 256 : b * 256 + 256].astype(BF16)
-                        hand_over(mix_out_1.at[b], (pair * 2 + b) * 2 + 1 - core)
-
-                @pl.when(n == 1)
-                def _():
-                    for b in range(2):
-                        part = mixt[:features, b * 256 : b * 256 + 256].astype(BF16)
-
-                        @pl.when(member == b)
-                        def _(part=part):
-                            mix_1[own_rows, :] = part
-
-                        @pl.when(member != b)
-                        def _(part=part):
-                            mix_out_1[2] = part
-                            hand_over(mix_out_1.at[2], there * 2 + core)
+                for par in range(2):
+                    part = mixt[:features, par * 256 : par * 256 + 256].astype(BF16)
+                    to_core = (par + x + 1) % 2
+
+                    @pl.when(n == 0)
+                    def _(par=par, part=part, to_core=to_core):
+                        mix_out_1[par] = part
+                        hand_over(mix_out_1.at[par], there * 2 + to_core)
+
+                    @pl.when(jnp.logical_and(n == 1, to_core == core))
+                    def _(part=part):
+                        mix_1[own_rows, :] = part
+
+                    @pl.when(jnp.logical_and(n == 1, to_core != core))
+                    def _(part=part):
+                        mix_out_1[2] = part
+                        hand_over(mix_out_1.at[2], sibling)
 
         if f == 0:
             forward(1)
@@ -296,28 +314,10 @@
                 finish(b, mix_0[:, pl.ds(pl.multiple_of(b * 256, 256), 256)])
 
             pl.semaphore_wait(all_in, 7)
-            targets = [((y + dy) % 4, dz, dy == 0) for dy, dz in YZ_FAR_FIRST]
+            send_first(0, YZ_FAR_FIRST)
         else:
             finish(member, mix_1[...])
-            targets = [(member * 2 + e, dz, True) for dz in (2, 1, 3, 0) for e in range(2)]
-
-        slot = i * 4 + y if f == 0 else 64 + i * 2 + pair
-        for chip, dz, may_be_here in targets:
-            for k in range(2):
-                for dc in range(2):
-                    to_x, to_z = (x + 1 + core + 2 * k) % 4, (z + dz) % 4
-                    dj = chip * 2 + (core + dc) % 2
-                    src = first_out.at[f, dj, to_x // 2 * 4 + to_z]
-                    copy = pltpu.make_async_remote_copy(
-                        src_ref=src, dst_ref=recv_t.at[slot], send_sem=send_b.at[f],
-                        recv_sem=recv_b.at[f], device_id=(to_x * 4 + to_z, dj), device_id_type=MESH,
-                    )
-                    if dz or dc or k == 0 or not may_be_here:
-                        copy.start()
-                    else:
-                        here = jnp.logical_and(core == 1, chip == y)
-                        pl.when(jnp.logical_not(here))(copy.start)
-                        pl.when(here)(pltpu.make_async_copy(src, recv_t.at[slot], recv_b.at[f]).start)
+            send_first(1, [(e, dz) for dz in (2, 1, 3, 0) for e in range(2)])
 
     lane96 = lax.broadcasted_iota(jnp.int32, (1, 96), 1)
     spatial(0)

time: 117 us -> 116 us (level)
  no operation moved by 1% of the time
where the time goes in v6:
time: 116 us; the launch traced here: 115 us
  Pallas kernels  113 us (97%)
  local copies, waits for them, and re-layouts  2.82 us (2%)
    pallas_call x1, Pallas kernels, body(): pl.pallas_call(kernel, out_shape=jax.ShapeDtypeStruct((6, 16, 8, D), BF16...  113 us
    unnamed x1, local copies, waits for them, and re-layouts  2.82 us

profile of v6, /device:TPU:0, one launch (start us, length us, event | category | flops | bytes accessed | tf_op | source)
XLA Modules:
  0.0 115.3 jit_solution(823305525197980474)
XLA Ops:
  0.0 112.5 %block.1 = bf16[6,16,8,1152]{3,2,1,0:T(8,128)(2,1)} custom-call(bf16[6,128,1152]{2,1,0:T(8,128)(2,1)} %tokens.1, s32[1,96]{1,0:T(1,128)} %bitcast.5, f32[6,4,1152]{2,1,0:T(4,128)} %bitcast.4, bf16[1152,3456]{1,0:T(8,128)(2,1)} %wsq.1, bf16[1152,1152]{1,0:T(8,128)(2,1)} %wso.1, bf16[1152,3456]{1,0:T(8,128)(2,1)} %wtq.1, bf16[1152,1152]{1,0:T(8,128)(2,1)} %wto.1), custom_call_target="tpu_custom_call" | custom-call | tf_op jit(solution)/shard_map/block/pallas_call | solution.py:434
  112.5 2.8 %copy.9 = bf16[6,128,1152]{2,1,0:T(8,128)(2,1)} copy(bf16[6,128,1152]{2,1,0:T(8,128)(2,1)} %bitcast.3) | data formatting | bytes 3538944

commit v7 on v6

--- a/solution.py
+++ b/solution.py
@@ -193,8 +193,7 @@
             for copy in head_columns(1):
                 copy.wait()
 
-        @pl.loop(0, 4)
-        def _(s):
+        def project_chip(s, e):
             yy = (y + jnp.where(s == 0, 0, jnp.where(s == 1, 2, jnp.where(s == 2, 1, 3)))) % 4
 
             if f == 0:
@@ -213,19 +212,27 @@
             qkv = dot(hidden, ws[:, : 3 * wide])
             q = (qkv[:, :wide] * Q_SCALE).reshape(2, 2, 2, 32, wide)
             for par in range(2):
-                qtf[:wide] = q[:, :, par].reshape(128, wide).T
+                qtf[2 * e + par, :wide] = q[:, :, par].reshape(128, wide).T
                 start = par * 512 + yy * 128 if f == 0 else yy // 2 * 512 + par * 256 + yy % 2 * 128
                 cols = pl.ds(pl.multiple_of(start, 128), 128)
                 for h in range(heads):
                     low, off = place(h)
                     row = lax.broadcasted_iota(jnp.int32, (WIN, 1), 0) + (off - low)
                     inside = jnp.logical_and(row >= 0, row < HD)
-                    qt_s[h, :, cols] = jnp.where(inside, qtf[pl.ds(off, WIN), :], 0.0).astype(BF16)
+                    qt_s[h, :, cols] = jnp.where(inside, qtf[2 * e + par, pl.ds(off, WIN), :], 0.0).astype(BF16)
             k_s[at, :wide] = qkv[:, wide : 2 * wide].astype(BF16)
-            vtf[:wide] = qkv[:, 2 * wide :].T
+            vtf[e, :wide] = qkv[:, 2 * wide :].T
             for h in range(heads):
                 low, _ = place(h)
-                vt_s[h, :HD, at] = vtf[pl.ds(pl.multiple_of(low, 8), HD), :].astype(BF16)
+                vt_s[h, :HD, at] = vtf[e, pl.ds(pl.multiple_of(low, 8), HD), :].astype(BF16)
+
+        @pl.loop(0, 4 if f == 0 else 2)
+        def _(u):
+            if f == 0:
+                project_chip(u, 0)
+            else:
+                project_chip(2 * u, 0)
+                project_chip(2 * u + 1, 1)
 
         if f == 0:
             for copy in head_columns(1):
@@ -234,9 +241,9 @@
         own_rows = pl.ds(pl.multiple_of(share * features, features), features)
         mix_f = mix_0 if f == 0 else mix_1
 
-        def hand_over(src, dest):
+        def hand_over(src, dest, rows=own_rows):
             pltpu.make_async_remote_copy(
-                src_ref=src, dst_ref=mix_f.at[own_rows], send_sem=send_m.at[f], recv_sem=recv_m.at[f],
+                src_ref=src, dst_ref=mix_f.at[rows], send_sem=send_m.at[f], recv_sem=recv_m.at[f],
                 device_id=(i, dest), device_id_type=MESH,
             ).start()
 
@@ -265,6 +272,16 @@
                 scores(jnp.minimum(2 * u + 2, heads - 1), 0)
                 attend(2 * u + 1, 1)
 
+                if f == 1:
+                    @pl.when(n == 0)
+                    def _():
+                        done = pl.ds(pl.multiple_of(u * 2 * HD, 2 * HD), 2 * HD)
+                        rows = pl.ds(pl.multiple_of(share * features + u * 2 * HD, 2 * HD), 2 * HD)
+                        for par in range(2):
+                            mix_out_1[par, done, :] = mixt[done, par * 256 : par * 256 + 256].astype(BF16)
+                            to_core = (par + x + 1) % 2
+                            hand_over(mix_out_1.at[par, done], (y + 1 - 2 * member) * 2 + to_core, rows)
+
             if f == 0:
                 @pl.when(n == 0)
                 def _():
@@ -275,15 +292,9 @@
                 def _():
                     mix_0[own_rows, :] = mixt[...].astype(BF16)
             else:
-                there = y + 1 - 2 * member
                 for par in range(2):
                     part = mixt[:features, par * 256 : par * 256 + 256].astype(BF16)
                     to_core = (par + x + 1) % 2
-
-                    @pl.when(n == 0)
-                    def _(par=par, part=part, to_core=to_core):
-                        mix_out_1[par] = part
-                        hand_over(mix_out_1.at[par], there * 2 + to_core)
 
                     @pl.when(jnp.logical_and(n == 1, to_core == core))
                     def _(part=part):
@@ -335,7 +346,7 @@
             for b in range(9):
                 f32_t[b, pl.ds(pl.multiple_of(base * 8 + c * 64, 64), 64), :] = rows[:, b * 128 : b * 128 + 128]
 
-        @pl.loop(0, 8)
+        @pl.loop(0, 8, unroll=4)
         def _(p, base=base, n=n, rows_f=rows_f):
             rows = jnp.concatenate([f32_t[b, pl.ds(base * 8 + p, n, stride=8), :] for b in range(9)], axis=1)
             at = pl.ds(pl.multiple_of(p * n, n), n)
@@ -442,8 +453,8 @@
             pltpu.VMEM((D, 1920), BF16),
             pltpu.VMEM((D, D), BF16),
             pltpu.VMEM((D, D), BF16),
-            pltpu.VMEM((640, 128), F32),
-            pltpu.VMEM((640, 256), F32),
+            pltpu.VMEM((4, 640, 128), F32),
+            pltpu.VMEM((2, 640, 256), F32),
             pltpu.VMEM((HEADS // 2, WIN, 1024), BF16),
             pltpu.VMEM((1024, 640), BF16),
             pltpu.VMEM((HEADS // 2, HD + 8, 1024), BF16),

time: 116 us -> 116 us (level)
  no operation moved by 1% of the time
where the time goes in v7:
time: 116 us; the launch traced here: 115 us
  Pallas kernels  112 us (97%)
  local copies, waits for them, and re-layouts  2.82 us (2%)
    pallas_call x1, Pallas kernels, body(): pl.pallas_call(kernel, out_shape=jax.ShapeDtypeStruct((6, 16, 8, D), BF16...  112 us
    unnamed x1, local copies, waits for them, and re-layouts  2.82 us

profile of v7, /device:TPU:0, one launch (start us, length us, event | category | flops | bytes accessed | tf_op | source)
XLA Modules:
  0.0 115.2 jit_solution(11186793877495528179)
XLA Ops:
  0.0 112.4 %block.1 = bf16[6,16,8,1152]{3,2,1,0:T(8,128)(2,1)} custom-call(bf16[6,128,1152]{2,1,0:T(8,128)(2,1)} %tokens.1, s32[1,96]{1,0:T(1,128)} %bitcast.5, f32[6,4,1152]{2,1,0:T(4,128)} %bitcast.4, bf16[1152,3456]{1,0:T(8,128)(2,1)} %wsq.1, bf16[1152,1152]{1,0:T(8,128)(2,1)} %wso.1, bf16[1152,3456]{1,0:T(8,128)(2,1)} %wtq.1, bf16[1152,1152]{1,0:T(8,128)(2,1)} %wto.1), custom_call_target="tpu_custom_call" | custom-call | tf_op jit(solution)/shard_map/block/pallas_call | solution.py:445
  112.4 2.8 %copy.9 = bf16[6,128,1152]{2,1,0:T(8,128)(2,1)} copy(bf16[6,128,1152]{2,1,0:T(8,128)(2,1)} %bitcast.3) | data formatting | bytes 3538944

commit v8 on v7

--- a/solution.py
+++ b/solution.py
@@ -265,12 +265,13 @@
 
             scores(0, 0)
 
-            @pl.loop(0, heads // 2)
+            several = 4 if f == 0 else 2
+
+            @pl.loop(0, heads // several)
             def _(u):
-                scores(2 * u + 1, 1)
-                attend(2 * u, 0)
-                scores(jnp.minimum(2 * u + 2, heads - 1), 0)
-                attend(2 * u + 1, 1)
+                for e in range(several):
+                    scores(jnp.minimum(several * u + e + 1, heads - 1), (e + 1) % 2)
+                    attend(several * u + e, e % 2)
 
                 if f == 1:
                     @pl.when(n == 0)
@@ -437,6 +438,18 @@
         pltpu.make_async_copy(recv_t.at[pl.ds(0, 6)], recv_t.at[pl.ds(0, 6)], send_c).wait()
 
     pltpu.make_async_copy(final, final, recv_c).wait()
+
+
+def copy_kernel(src, out, buf, in_sem, out_sem):
+    ins = [pltpu.make_async_copy(src.at[n], buf.at[n], in_sem.at[n]) for n in range(6)]
+    outs = [pltpu.make_async_copy(buf.at[n], out.at[n], out_sem.at[n]) for n in range(6)]
+    for copy in ins:
+        copy.start()
+    for arriving, leaving in zip(ins, outs):
+        arriving.wait()
+        leaving.start()
+    for copy in outs:
+        copy.wait()
 
 
 def body(tokens, clip_ids, modulation, w_spatial_qkv, w_spatial_out, w_temporal_qkv, w_temporal_out):
@@ -484,7 +497,15 @@
         tokens, clip_ids.reshape(1, 96), modulation.transpose(1, 0, 2),
         w_spatial_qkv, w_spatial_out, w_temporal_qkv, w_temporal_out,
     )
-    return final.reshape(6, 128, D)
+    return pl.pallas_call(
+        copy_kernel,
+        out_shape=jax.ShapeDtypeStruct((6, 128, D), BF16),
+        in_specs=[any_],
+        out_specs=any_,
+        scratch_shapes=[pltpu.VMEM((6, 128, D), BF16), dma((6,)), dma((6,))],
+        compiler_params=pltpu.CompilerParams(vmem_limit_bytes=63 * 1024 * 1024),
+        name="result",
+    )(final.reshape(6, 128, D))
 
 
 def solution(mesh):

time: 116 us -> 115 us (level)
  local copies, waits for them, and re-layouts: 2.82 us -> 0 us
  Pallas kernels: 112 us -> 114 us
    unnamed x1 -> x0, local copies, waits for them, and re-layouts: 2.82 us -> none
    pallas_call x0 -> x1, Pallas kernels: none -> 2.27 us  [body(): pl.pallas_call(copy_kernel, out_shape=jax.ShapeDtypeStruct((6, 128, D), B...]
where the time goes in v8:
time: 115 us; the launch traced here: 114 us
  Pallas kernels  114 us (99%)
    pallas_call x1, Pallas kernels, body(): pl.pallas_call(kernel, out_shape=jax.ShapeDtypeStruct((6, 16, 8, D), BF16...  112 us

profile of v8, /device:TPU:0, one launch (start us, length us, event | category | flops | bytes accessed | tf_op | source)
XLA Modules:
  0.0 114.2 jit_solution(18165451880711079025)
XLA Ops:
  0.0 111.7 %block.1 = bf16[6,16,8,1152]{3,2,1,0:T(8,128)(2,1)} custom-call(bf16[6,128,1152]{2,1,0:T(8,128)(2,1)} %tokens.1, s32[1,96]{1,0:T(1,128)} %bitcast.5, f32[6,4,1152]{2,1,0:T(4,128)} %bitcast.4, bf16[1152,3456]{1,0:T(8,128)(2,1)} %wsq.1, bf16[1152,1152]{1,0:T(8,128)(2,1)} %wso.1, bf16[1152,3456]{1,0:T(8,128)(2,1)} %wtq.1, bf16[1152,1152]{1,0:T(8,128)(2,1)} %wto.1), custom_call_target="tpu_custom_call" | custom-call | tf_op jit(solution)/shard_map/block/pallas_call | solution.py:458
  111.7 2.3 %result.1 = bf16[6,128,1152]{2,1,0:T(8,128)(2,1)} custom-call(bf16[6,128,1152]{2,1,0:T(8,128)(2,1)} %bitcast.3), custom_call_target="tpu_custom_call" | custom-call | tf_op jit(solution)/shard_map/result/pallas_call | solution.py:500
